TPU v7x, 256 devices: a whole 4x4x8 slice. The times are simulated.
256 devices in a mesh: dp: 2 (over core), fsdp: 4 (over x), tensor: 32 (over z, y).
Axes of the slice: x: 4, y: 4, z: 8, core: 2. Of those that a mesh axis runs over, the one named last changes fastest.
Arguments:
- gradients: bfloat16 [2, 32, 1024, 1024], P('dp', 'fsdp', 'tensor')
- owner_lists: int32 [4, 8], P('fsdp'), may hold values from 0 to 1, as said below
- left_stats: float32 [2, 4, 6, 1024, 1024], P('dp', 'fsdp', None, 'tensor')
- right_stats: float32 [2, 4, 6, 1024, 1024], P('dp', 'fsdp', None, 'tensor')
- left_roots: bfloat16 [2, 4, 6, 1024, 1024], P('dp', 'fsdp', None, 'tensor'), as said below
- right_roots: bfloat16 [2, 4, 6, 1024, 1024], P('dp', 'fsdp', None, 'tensor'), as said below
Outputs:
- new_left: float32 [2, 4, 6, 1024, 1024], P('dp', 'fsdp', None, 'tensor')
- new_right: float32 [2, 4, 6, 1024, 1024], P('dp', 'fsdp', None, 'tensor')
- updates: bfloat16 [32, 1024, 1024], P('fsdp', 'tensor')
Inputs may be any that keep to these rules, and one draw needn't show every extreme that they name: `owner_lists`: each index of dp owns at most 6 of the blocks of one index of fsdp, and in every row one index owns exactly 6. Every block of left_roots is symmetric. Every block of right_roots is symmetric.
All inputs are finite; a program needn't handle non-finite values.
Results may differ from a plain program's by a relative error of at most 0.017.
Values may be sent and summed in bfloat16 or wider, within the bound.
A program may use at most 128 MiB of HBM per device.

v0:
```python
import math

import jax
import jax.numpy as jnp
from jax import lax
from jax.sharding import PartitionSpec as P

STAT_DECAY = 0.9


def on_device(gradients, owner_lists, left_stats, right_stats, left_roots, right_roots):
    replica_count = lax.axis_size("dp")
    own_index = lax.axis_index("dp")
    block_count = gradients.shape[1]
    row_count = gradients.shape[2]
    block_width = gradients.shape[3]
    slot_count = left_stats.shape[2]
    local_grads = gradients[0]
    owner_row = owner_lists[0]
    positions = jnp.arange(block_count)
    same_owner = owner_row[:, None] == owner_row[None, :]
    slot_rank = jnp.sum(same_owner & (positions[None, :] < positions[:, None]), axis=1)
    slot_hot = slot_rank[None, :] == jnp.arange(slot_count)[:, None]
    mine_hot = slot_hot & (owner_row[None, :] == own_index)
    owned_slot = jnp.any(mine_hot, axis=1)
    send_hot = (owner_row[None, None, :] == jnp.arange(replica_count)[:, None, None]) & slot_hot[
        None
    ]
    buffer = jnp.einsum(
        "ock,krb->ocrb",
        send_hot.astype(jnp.bfloat16),
        local_grads,
        preferred_element_type=jnp.float32,
    )
    buffer = buffer.reshape(replica_count * slot_count, row_count, block_width)
    owned = lax.psum_scatter(
        buffer.astype(jnp.bfloat16), "dp", scatter_dimension=0, tiled=True
    ).astype(jnp.float32)
    squares = lax.psum(jnp.sum(owned * owned), ("dp", "fsdp", "tensor"))
    clip_limit = 2.0 * math.sqrt(lax.axis_size("fsdp") * block_count * block_width * block_width)
    factor = jnp.minimum(jnp.float32(1.0), clip_limit / (jnp.sqrt(squares) + 1e-06))
    scaled = (owned * factor).astype(jnp.bfloat16)
    row_offset = lax.axis_index("tensor") * row_count
    left_rows = left_roots[0, 0]
    piece_rows = lax.all_gather(scaled, "tensor", axis=1, tiled=True)
    block_left = jnp.einsum("csk,cnk->csn", scaled, piece_rows, preferred_element_type=jnp.float32)
    gram_left = block_left
    piece_cols = lax.dynamic_slice_in_dim(piece_rows, row_offset, row_count, 2)
    gram_right = jnp.einsum(
        "cnr,cnk->crk", piece_cols, piece_rows, preferred_element_type=jnp.float32
    )
    applied = jnp.einsum("csn,cnk->csk", left_rows, piece_rows, preferred_element_type=jnp.float32)
    gram_left, gram_right, applied = (gram_left, gram_right, applied)
    mix_new = (1.0 - STAT_DECAY) / block_width
    keep_mask = owned_slot[:, None, None]
    new_left = jnp.where(
        keep_mask, STAT_DECAY * left_stats[0, 0] + mix_new * gram_left, left_stats[0, 0]
    )
    new_right = jnp.where(
        keep_mask, STAT_DECAY * right_stats[0, 0] + mix_new * gram_right, right_stats[0, 0]
    )
    applied_low = applied.astype(jnp.bfloat16)
    update_rows = jnp.einsum(
        "csk,cnk->csn",
        applied_low,
        lax.all_gather(right_roots[0, 0], "tensor", axis=1, tiled=True),
        preferred_element_type=jnp.float32,
    ).astype(jnp.bfloat16)
    gathered = lax.all_gather(update_rows[None], "dp", axis=0, tiled=True)
    gathered = gathered.reshape(replica_count * slot_count, row_count, block_width)
    read_hot = send_hot.reshape(replica_count * slot_count, block_count).T.astype(jnp.bfloat16)
    updates = jnp.einsum(
        "kq,qrb->krb", read_hot, gathered, preferred_element_type=jnp.float32
    ).astype(jnp.bfloat16)
    return (new_left[None, None], new_right[None, None], updates)


def solution(mesh):
    placed = (
        P("dp", "fsdp", "tensor", None),
        P("fsdp", None),
        P("dp", "fsdp", None, "tensor", None),
        P("dp", "fsdp", None, "tensor", None),
        P("dp", "fsdp", None, "tensor", None),
        P("dp", "fsdp", None, "tensor", None),
    )
    return jax.shard_map(
        on_device,
        mesh=mesh,
        in_specs=placed,
        out_specs=(
            P("dp", "fsdp", None, "tensor", None),
            P("dp", "fsdp", None, "tensor", None),
            P("fsdp", "tensor", None),
        ),
        check_vma=False,
    )
```

profile of v0, /device:TPU:1, one launch (start us, length us, event | category | flops | bytes accessed | tf_op | source)
XLA Modules:
  0.0 298.7 jit_solution(15389364723446390051)
XLA Ops:
  8.0 0.0 copy-start
  8.0 0.0 reduce-scatter.2.cloned.1.call-start
  8.1 0.7 iota_compare_fusion.2
  8.8 0.9 convert_reduce_fusion
  9.7 0.7 compare_bitcast_fusion
  10.3 0.1 and_reduce_fusion
  10.5 0.0 copy-done
  10.5 0.4 convolution_convert_fusion
  11.0 1.3 copy.43
  12.3 0.0 reduce-scatter.2.cloned.1.call-update
  12.3 0.0 all-gather.7.cloned.1.call-start
  12.3 0.5 all-gather.7.cloned.1.call-update
  12.9 0.0 all-gather.5.cloned.1.call-start
  12.9 17.7 %reduce-scatter.2.cloned.1.call-done = bf16[6,32,1024]{2,1,0:T(8,128)(2,1)} async-done(((bf16[12,32,1024]{2,1,0:T(8,128)(2,1)}), bf16[6,32,1024]{2,1,0:T(8,128)(2,1)}) %reduce-scatter.2.cloned.1.call-update) | async-done | bytes 393232 | tf_op jit(solution)/shard_map/reduce_scatter | solution.py:36
  30.6 1.8 fusion.24
  32.4 79.5 %psum.7 = f32[]{:T(128)} all-reduce(f32[]{:T(128)} %fusion.24), channel_id=1, replica_groups=mesh['dp'=2,'fsdp'=4,'tensor'=32] {'dp','fsdp','tensor'}, use_global_device_ids=true, to_apply=%region_4.0 | all-reduce | flops 1 | bytes 8 | tf_op jit(solution)/shard_map/psum | solution.py:39
  112.7 1.8 fusion.25
  114.5 0.0 all-gather.5.cloned.1.call-update
  114.5 0.0 copy-start.2
  114.5 0.0 copy-start.3
  114.5 24.5 %all-gather.7.cloned.1.call-done = bf16[1,1,6,1024,1024]{4,3,2,1,0:T(8,128)(2,1)} async-done(((bf16[1,1,6,32,1024]{4,3,2,1,0:T(8,128)(2,1)}), bf16[1,1,6,1024,1024]{4,3,2,1,0:T(8,128)(2,1)}) %all-gather.7.cloned.1.call-update) | async-done | bytes 12582928 | tf_op jit(solution)/shard_map/all_gather | solution.py:66
  139.1 119.5 %all-gather.5.cloned.1.call-done = bf16[6,1024,1024]{2,1,0:T(8,128)(2,1)} async-done(((bf16[6,32,1024]{2,1,0:T(8,128)(2,1)}), bf16[6,1024,1024]{2,1,0:T(8,128)(2,1)}) %all-gather.5.cloned.1.call-update) | async-done | bytes 12582928 | tf_op jit(solution)/shard_map/all_gather | solution.py:45
  258.6 14.2 %fusion.20 = bf16[6,32,1024]{2,1,0:T(8,128)(2,1)S(1)} fusion(bf16[1,1,6,1024,1024]{4,3,2,1,0:T(8,128)(2,1)} %all-gather.7.cloned.1.call-done, bf16[6,1024,1024]{2,1,0:T(8,128)(2,1)} %all-gather.5.cloned.1.call-done, bf16[1,1,6,32,1024]{4,3,2,1,0:T(8,128)(2,1)} %param.10), kind=kOutput, calls=%fused_computation.15 | convolution fusion | flops 805699584 | bytes 25952256 | tf_op jit(solution)/shard_map/csk,cnk->csn/dot_general | solution.py:63
  272.9 0.0 copy-start.1
  272.9 0.0 copy-start.4
  272.9 3.5 %all-gather.1 = bf16[12,32,1024]{2,1,0:T(8,128)(2,1)S(1)} all-gather(bf16[6,32,1024]{2,1,0:T(8,128)(2,1)S(1)} %fusion.20), channel_id=3, replica_groups=mesh['dp'=2,'fsdp'=4,'tensor'=32] {'dp'}, dimensions={0}, use_global_device_ids=true | all-gather | bytes 1179648 | tf_op jit(solution)/shard_map/all_gather | solution.py:69
  276.4 1.0 fusion.4
  277.4 1.1 copy.47
  278.5 0.0 copy-done.2
  278.5 9.3 %fusion.7 = f32[1,1,6,32,1024]{4,3,2,1,0:T(8,128)} fusion(bf16[6,32,1024]{2,1,0:T(8,128)(2,1)S(1)} %copy-done.2, bf16[6,1024,1024]{2,1,0:T(8,128)(2,1)} %all-gather.5.cloned.1.call-done, f32[1,1,6,32,1024]{4,3,2,1,0:T(8,128)S(1)} %copy-done.3, pred[6]{0:T(512)(128)(4,1)S(1)} %get-tuple-element.18), kind=kOutput, calls=%fused_computation.10 | convolution fusion | flops 403439616 | bytes 14548998 | tf_op jit(solution)/shard_map/csk,cnk->csn/dot_general | solution.py:46
  287.8 0.0 copy-done.1
  287.8 3.5 %fusion.17 = f32[1,1,6,32,1024]{4,3,2,1,0:T(8,128)} fusion(bf16[6,1024,1024]{2,1,0:T(8,128)(2,1)S(1)} %copy-done.1, s32[]{:T(128)S(6)} %select_n.11, f32[1,1,6,32,1024]{4,3,2,1,0:T(8,128)S(1)} %copy-done.4, pred[6]{0:T(512)(128)(4,1)S(1)} %get-tuple-element.18), kind=kOutput, calls=%fused_computation.14 | convolution fusion | flops 403439616 | bytes 15729156 | tf_op jit(solution)/shard_map/cnr,cnk->crk/dot_general | solution.py:49
  (4 shorter events, 0.0 us)
Async XLA Ops:
  8.0 2.5 copy-start
  8.0 22.6 %reduce-scatter.2.cloned.1.call-start = ((), (), s32[]{:S(2)}) async-start(), calls=%async_computation.1 | async-start | bytes 1179648 | tf_op jit(solution)/shard_map/reduce_scatter | solution.py:36
  12.3 126.8 %all-gather.7.cloned.1.call-start = ((), (), s32[]{:S(2)}) async-start(), calls=%async_computation.3 | async-start | bytes 12976128 | tf_op jit(solution)/shard_map/all_gather | solution.py:66
  12.9 245.7 %all-gather.5.cloned.1.call-start = ((), (), s32[]{:S(2)}) async-start(), calls=%async_computation.2 | async-start | bytes 12976128 | tf_op jit(solution)/shard_map/all_gather | solution.py:45
  114.5 163.9 %copy-start.2 = (bf16[6,32,1024]{2,1,0:T(8,128)(2,1)S(1)}, bf16[6,32,1024]{2,1,0:T(8,128)(2,1)}, u32[]{:S(2)}) copy-start(bf16[6,32,1024]{2,1,0:T(8,128)(2,1)} %fusion.25) | copy-start | bytes 1179652
  114.5 163.9 %copy-start.3 = (f32[1,1,6,32,1024]{4,3,2,1,0:T(8,128)S(1)}, f32[1,1,6,32,1024]{4,3,2,1,0:T(8,128)}, u32[]{:S(2)}) copy-start(f32[1,1,6,32,1024]{4,3,2,1,0:T(8,128)} %param.8) | copy-start | bytes 2359300
  272.9 14.9 %copy-start.1 = (bf16[6,1024,1024]{2,1,0:T(8,128)(2,1)S(1)}, bf16[6,1024,1024]{2,1,0:T(8,128)(2,1)}, u32[]{:S(2)}) copy-start(bf16[6,1024,1024]{2,1,0:T(8,128)(2,1)} %all-gather.5.cloned.1.call-done) | copy-start | bytes 37748740
  272.9 14.9 %copy-start.4 = (f32[1,1,6,32,1024]{4,3,2,1,0:T(8,128)S(1)}, f32[1,1,6,32,1024]{4,3,2,1,0:T(8,128)}, u32[]{:S(2)}) copy-start(f32[1,1,6,32,1024]{4,3,2,1,0:T(8,128)} %param.9) | copy-start | bytes 2359300
Sparse Core Ops, SparseCore 0:
  12.4 18.1 reduce-scatter.1
Sparse Core Ops, SparseCore 1:
  15.7 123.3 all-gather.6
  142.4 116.1 all-gather.4
where the time goes:
time: 299 us
  waiting for transfers between devices  162 us (54%)
  blocking collectives  83 us (28%)
  matrix products  28.5 us (10%)
  between operations  16.3 us (5%)
  other arithmetic  6.07 us (2%)
    all_gather x1, waiting for transfers between devices, on_device(): piece_rows = lax.all_gather(scaled, 'tensor', axis=1, tiled=True)  120 us
    psum x1, blocking collectives, on_device(): squares = lax.psum(jnp.sum(owned * owned), ('dp', 'fsdp', 'tensor'))  79.5 us
    all_gather x1, waiting for transfers between devices, on_device(): lax.all_gather(right_roots[0, 0], 'tensor', axis=1, tiled=True)  24.5 us
    reduce_scatter x1, waiting for transfers between devices, on_device(): lax.psum_scatter(buffer.astype(jnp.bfloat16), 'dp', scatter_dimension=0,...  17.7 us
    dot_general x1, matrix products, on_device(): jnp.einsum('csk,cnk->csn', applied_low, lax.all_gather(right_roots[0, 0],...  14.2 us
    dot_general x1, matrix products, on_device(): jnp.einsum('csk,cnk->csn', scaled, piece_rows, preferred_element_type=jnp...  9.29 us
  transfers between devices with their start and end apart: 3, of which 3 were waited for; matrix products, arithmetic and copies ran while one was open for 1% of the time, Pallas kernels for 0%

commit v1 on v0

v1 whole, which is shorter than its diff:
```python
import functools
import math

import jax
import jax.numpy as jnp
from jax import lax
from jax.experimental import pallas as pl
from jax.experimental.pallas import tpu as pltpu
from jax.sharding import PartitionSpec as P

STAT_DECAY = 0.9
MESH = pl.DeviceIdType.MESH
NZ = 8
NY = 4
NX = 4
HALF = 16
WIDTH = 1024
KF = 8
SLOTS = 6
BF16 = jnp.bfloat16
F32 = jnp.float32


def kernel(
    owner_ref, grad_ref, lstat_ref, rstat_ref, lroot_ref, rroot_ref,
    nleft_ref, nright_ref, upd_ref,
    own_g, got_g, part, lboth, rboth, lpart, rpart, lmine, gall, rall, lhs, lhs2, app,
    norm_z, norm_y, norm_x, norm_c,
    out_s, out_r0, out_r1, out_r2, lst, rst,
    loc_sem, c_ssem, c_rsem, z_ssem, z_rsem, y_ssem, y_rsem, f_ssem, f_rsem,
    n_ssem, n_rsem, o_ssem, o_rsem, fin_sem,
):
    out_r = (out_r0, out_r1, out_r2)
    c = lax.axis_index("dp")
    x = lax.axis_index("fsdp")
    t = lax.axis_index("tensor")
    z, y = t // NY, t % NY
    oc = 1 - c

    def at_z(d):
        return {"tensor": lax.rem(z + d, NZ) * NY + y}

    def at_y(d):
        return {"tensor": z * NY + lax.rem(y + d, NY)}

    def at_x(d):
        return {"fsdp": lax.rem(x + d, NX)}

    at_c = {"dp": oc}

    def remote(src, dst, ssem, rsem, device):
        return pltpu.make_async_remote_copy(
            src_ref=src, dst_ref=dst, send_sem=ssem, recv_sem=rsem,
            device_id=device, device_id_type=MESH,
        )

    local = [
        pltpu.make_async_copy(grad_ref.at[:, c], own_g, loc_sem.at[0]),
        pltpu.make_async_copy(lroot_ref.at[:, c], lboth.at[c], loc_sem.at[1]),
        pltpu.make_async_copy(rroot_ref.at[:, c], rboth.at[c], loc_sem.at[2]),
        pltpu.make_async_copy(lstat_ref, lst, loc_sem.at[3]),
        pltpu.make_async_copy(rstat_ref, rst, loc_sem.at[4]),
    ]
    for copy in local:
        copy.start()

    peers = (
        [at_z(d) for d in range(1, NZ)]
        + [at_y(d) for d in range(1, NY)]
        + [at_x(d) for d in range(1, NX)]
        + [at_c]
    )
    barrier = pltpu.get_barrier_semaphore()
    for peer in peers:
        pl.semaphore_signal(barrier, inc=1, device_id=peer, device_id_type=MESH)
    pl.semaphore_wait(barrier, len(peers))

    halves = [
        remote(grad_ref.at[:, oc], got_g, c_ssem.at[0], c_rsem.at[0], at_c),
        remote(lroot_ref.at[:, oc], lboth.at[c], c_ssem.at[1], c_rsem.at[1], at_c),
        remote(rroot_ref.at[:, oc], rboth.at[c], c_ssem.at[2], c_rsem.at[2], at_c),
    ]
    for copy in halves:
        copy.start()

    owners = [owner_ref[j] for j in range(KF)]
    ranks = []
    for j in range(KF):
        rank = jnp.int32(0)
        for i in range(j):
            rank += jnp.where(owners[i] == owners[j], 1, 0).astype(jnp.int32)
        ranks.append(jnp.minimum(rank, SLOTS - 1))

    local[0].wait()
    halves[0].wait_recv()
    squares = jnp.zeros((HALF, WIDTH), F32)
    for j in range(KF):
        total = own_g[j].astype(F32) + got_g[j].astype(F32)
        part[j] = total.astype(BF16)
        squares += total * total

    def z_sends(k, src, dst):
        return [
            remote(
                src.at[lax.rem(z + d, NZ)], dst, z_ssem.at[k, d], z_rsem.at[k, d], at_z(d)
            )
            for d in range(1, NZ)
        ]

    g_z = z_sends(0, part, gall.at[z, y, c])
    for copy in g_z:
        copy.start()
    gall[z, y, c] = part[z]

    norm_z[z] = jnp.full((8, 128), jnp.sum(squares), F32)
    n_z = [
        remote(norm_z.at[z], norm_z.at[z], n_ssem.at[0, d], n_rsem.at[0, d], at_z(d))
        for d in range(1, NZ)
    ]
    for copy in n_z:
        copy.start()

    local[1].wait()
    halves[1].wait_recv()
    for j in range(KF):
        lpart[j] = lboth[owners[j], ranks[j]]
    local[2].wait()
    halves[2].wait_recv()
    for j in range(KF):
        rpart[j] = rboth[owners[j], ranks[j]]
    lmine[z] = lpart[z]
    rall[z, y, c] = rpart[z]

    row = lax.broadcasted_iota(jnp.int32, (128, WIDTH), 0)
    col = lax.broadcasted_iota(jnp.int32, (128, WIDTH), 1)
    pick = (row // HALF) * 128 + y * 32 + c * HALF + row % HALF
    lhs[pl.ds(128, 128), :] = jnp.where(col == pick, 1.0, 0.0).astype(BF16)

    for copy in n_z:
        copy.wait_recv()
    norm_y[y] = jnp.sum(norm_z[...], axis=0)
    n_y = [
        remote(norm_y.at[y], norm_y.at[y], n_ssem.at[1, d], n_rsem.at[1, d], at_y(d))
        for d in range(1, NY)
    ]
    for copy in n_y:
        copy.start()

    for copy in g_z:
        copy.wait_recv()

    def y_sends(k, buf):
        own = buf.at[:, y, c]
        return [
            remote(own, own, y_ssem.at[k, d], y_rsem.at[k, d], at_y(d)) for d in range(1, NY)
        ]

    def forwards(k, buf):
        return [
            remote(
                buf.at[:, lax.rem(y + NY - d, NY), c], buf.at[:, lax.rem(y + NY - d, NY), c],
                f_ssem.at[k, d], f_rsem.at[k, d], at_c,
            )
            for d in range(NY)
        ]

    g_y = y_sends(0, gall)
    for copy in g_y:
        copy.start()
    g_f = forwards(0, gall)
    g_f[0].start()

    l_z = z_sends(1, lpart, lmine.at[z])
    r_z = z_sends(2, rpart, rall.at[z, y, c])
    for copy in l_z + r_z:
        copy.start()

    for copy in n_y:
        copy.wait_recv()
    norm_x[x] = jnp.sum(norm_y[...], axis=0)
    n_x = [
        remote(norm_x.at[x], norm_x.at[x], n_ssem.at[2, d], n_rsem.at[2, d], at_x(d))
        for d in range(1, NX)
    ]
    for copy in n_x:
        copy.start()
    for copy in n_x:
        copy.wait_recv()
    norm_c[c] = jnp.sum(norm_x[...], axis=0)
    n_c = remote(norm_c.at[c], norm_c.at[c], n_ssem.at[3, 0], n_rsem.at[3, 0], at_c)
    n_c.start()
    n_c.wait_recv()
    clip = 2.0 * math.sqrt(NX * KF * WIDTH * WIDTH)
    norm = jnp.sqrt(norm_c[0] + norm_c[1])
    factor = jnp.minimum(jnp.float32(1.0), clip / (norm + 1e-06))[0:1, 0:1]

    for d in (1, 3, 2):
        g_y[d - 1].wait_recv()
        g_f[d].start()

    for copy in l_z + r_z:
        copy.wait_recv()
    r_y = y_sends(1, rall)
    for copy in r_y:
        copy.start()
    r_f = forwards(1, rall)
    r_f[0].start()

    for copy in g_f:
        copy.wait()
    for copy in g_y:
        copy.wait_send()

    for i in range(NZ):
        gall[i] = (gall[i].astype(F32) * factor).astype(BF16)

    lhs[pl.ds(0, 128), :] = gall[:, y, c].reshape(128, WIDTH)
    lhs2[pl.ds(128, 128), :] = lmine[...].reshape(128, WIDTH)

    def o_sends(k):
        return [
            remote(
                out_s.at[k, lax.rem(z + d, NZ)], out_r[k].at[z, c],
                z_ssem.at[3 + k, d], z_rsem.at[3 + k, d], at_z(d),
            )
            for d in range(1, NZ)
        ]

    nt = (((1,), (1,)), ((), ()))
    for n in range(4):
        g_rows = gall[pl.ds(2 * n, 2)].reshape(256, WIDTH)
        both = lax.dot_general(lhs[...], g_rows, nt, preferred_element_type=F32).astype(BF16)
        out_s[0, :, :, pl.ds(256 * n, 256)] = both[:128].reshape(NZ, HALF, 256)
        lhs2[pl.ds(0, 128), pl.ds(256 * n, 256)] = both[128:]
    o_left = o_sends(0)
    for copy in o_left:
        copy.start()
    for n in range(4):
        g_cols = gall[:, :, :, :, pl.ds(256 * n, 256)].reshape(WIDTH, 256)
        both = jnp.dot(lhs2[...], g_cols, preferred_element_type=F32).astype(BF16)
        out_s[1, :, :, pl.ds(256 * n, 256)] = both[:128].reshape(NZ, HALF, 256)
        app[:, pl.ds(256 * n, 256)] = both[128:]
    o_right = o_sends(1)
    for copy in o_right:
        copy.start()

    for d in (1, 3, 2):
        r_y[d - 1].wait_recv()
        r_f[d].start()
    for copy in r_f:
        copy.wait()
    for copy in r_y:
        copy.wait_send()
    for n in range(4):
        r_cols = rall[:, :, :, :, pl.ds(256 * n, 256)].reshape(WIDTH, 256)
        upd = jnp.dot(app[...], r_cols, preferred_element_type=F32).astype(BF16)
        out_s[2, :, :, pl.ds(256 * n, 256)] = upd.reshape(NZ, HALF, 256)
    o_upd = o_sends(2)
    for copy in o_upd:
        copy.start()
    for k in range(3):
        out_r[k][z, c] = out_s[k, z]

    def finish(k, sends):
        shared = []
        for d in range(NZ):
            if d:
                sends[d - 1].wait_recv()
            here = out_r[k].at[lax.rem(z + NZ - d, NZ), c]
            copy = remote(here, here, o_ssem.at[k, d], o_rsem.at[k, d], at_c)
            copy.start()
            shared.append(copy)
        for copy in shared:
            copy.wait()
        for copy in sends:
            copy.wait_send()

    places, taken = [], []
    for s in range(SLOTS):
        place, count = jnp.int32(0), jnp.int32(0)
        for j in range(KF):
            hit = (owners[j] == c) & (ranks[j] == s)
            place = jnp.where(hit, j, place)
            count = jnp.where(hit, 1, count)
        places.append(place)
        taken.append(count)

    mix = (1.0 - STAT_DECAY) / WIDTH

    def stats(k, buf, out_ref):
        for s in range(SLOTS):
            gram = out_r[k][places[s]].astype(F32)
            new = STAT_DECAY * buf[s] + mix * gram
            buf[s] = jnp.where(taken[s] > 0, new, buf[s])
        copy = pltpu.make_async_copy(buf, out_ref, fin_sem.at[k])
        copy.start()
        return copy

    local[3].wait()
    finish(0, o_left)
    done_left = stats(0, lst, nleft_ref)
    local[4].wait()
    finish(1, o_right)
    done_right = stats(1, rst, nright_ref)
    finish(2, o_upd)
    done_upd = pltpu.make_async_copy(out_r2, upd_ref, fin_sem.at[2])
    done_upd.start()

    for copy in halves + g_z + l_z + r_z + n_z + n_y + n_x + [n_c]:
        copy.wait_send()
    for copy in (done_left, done_right, done_upd):
        copy.wait()


def on_device(gradients, owner_lists, left_stats, right_stats, left_roots, right_roots):
    any_space = pl.BlockSpec(memory_space=pl.ANY)
    vmem, dma = pltpu.VMEM, pltpu.SemaphoreType.DMA
    stat_shape = (SLOTS, 2, HALF, WIDTH)
    new_left, new_right, updates = pl.pallas_call(
        kernel,
        out_shape=[
            jax.ShapeDtypeStruct(stat_shape, F32),
            jax.ShapeDtypeStruct(stat_shape, F32),
            jax.ShapeDtypeStruct((KF, 2, HALF, WIDTH), BF16),
        ],
        in_specs=[pl.BlockSpec(memory_space=pltpu.SMEM)] + [any_space] * 5,
        out_specs=[any_space] * 3,
        scratch_shapes=[
            vmem((KF, HALF, WIDTH), BF16),
            vmem((KF, HALF, WIDTH), BF16),
            vmem((KF, HALF, WIDTH), BF16),
            vmem((2, SLOTS, HALF, WIDTH), BF16),
            vmem((2, SLOTS, HALF, WIDTH), BF16),
            vmem((KF, HALF, WIDTH), BF16),
            vmem((KF, HALF, WIDTH), BF16),
            vmem((NZ, HALF, WIDTH), BF16),
            vmem((NZ, NY, 2, HALF, WIDTH), BF16),
            vmem((NZ, NY, 2, HALF, WIDTH), BF16),
            vmem((256, WIDTH), BF16),
            vmem((256, WIDTH), BF16),
            vmem((128, WIDTH), BF16),
            vmem((NZ, 8, 128), F32),
            vmem((NY, 8, 128), F32),
            vmem((NX, 8, 128), F32),
            vmem((2, 8, 128), F32),
            vmem((3, NZ, HALF, WIDTH), BF16),
            vmem((KF, 2, HALF, WIDTH), BF16),
            vmem((KF, 2, HALF, WIDTH), BF16),
            vmem((KF, 2, HALF, WIDTH), BF16),
            vmem(stat_shape, F32),
            vmem(stat_shape, F32),
            dma((5,)),
            dma((3,)), dma((3,)),
            dma((6, NZ)), dma((6, NZ)),
            dma((2, NY)), dma((2, NY)),
            dma((2, NY)), dma((2, NY)),
            dma((4, NZ)), dma((4, NZ)),
            dma((3, NZ)), dma((3, NZ)),
            dma((3,)),
        ],
        compiler_params=pltpu.CompilerParams(
            collective_id=0, has_side_effects=True, vmem_limit_bytes=60 * 2**20
        ),
    )(
        owner_lists[0],
        gradients.reshape(KF, 2, HALF, WIDTH),
        left_stats.reshape(stat_shape),
        right_stats.reshape(stat_shape),
        left_roots.reshape(stat_shape),
        right_roots.reshape(stat_shape),
    )
    full = (1, 1, SLOTS, 2 * HALF, WIDTH)
    return (
        new_left.reshape(full),
        new_right.reshape(full),
        updates.reshape(KF, 2 * HALF, WIDTH),
    )


def solution(mesh):
    placed = (
        P("dp", "fsdp", "tensor", None),
        P("fsdp", None),
        P("dp", "fsdp", None, "tensor", None),
        P("dp", "fsdp", None, "tensor", None),
        P("dp", "fsdp", None, "tensor", None),
        P("dp", "fsdp", None, "tensor", None),
    )
    return jax.shard_map(
        on_device,
        mesh=mesh,
        in_specs=placed,
        out_specs=(
            P("dp", "fsdp", None, "tensor", None),
            P("dp", "fsdp", None, "tensor", None),
            P("fsdp", "tensor", None),
        ),
        check_vma=False,
    )
```

time: 299 us -> 69.5 us (0.23)
  waiting for transfers between devices: 162 us -> 0 us
  blocking collectives: 83 us -> 0 us
  Pallas kernels: 0 us -> 64.4 us
  matrix products: 28.5 us -> 0 us
  between operations: 16.3 us -> 0.65 us
  other arithmetic: 6.07 us -> 0 us
    all_gather x2 -> x0, waiting for transfers between devices: 144 us -> none  [the longest x1 120 us: on_device(): piece_rows = lax.all_gather(scaled, 'tensor', axis=1, tiled=True)]
    psum x1 -> x0, blocking collectives: 79.5 us -> none  [on_device(): squares = lax.psum(jnp.sum(owned * owned), ('dp', 'fsdp', 'tensor'))]
    pallas_call x0 -> x1, Pallas kernels: none -> 64.4 us  [on_device(): pl.pallas_call(kernel, out_shape=[jax.ShapeDtypeStruct(stat_shape, F32),...]
    dot_general x5 -> x0, matrix products: 28.5 us -> none  [the longest x1 14.2 us: on_device(): jnp.einsum('csk,cnk->csn', applied_low, lax.all_gather(right_roots[0, 0],...]
    reduce_scatter x1 -> x0, waiting for transfers between devices: 17.7 us -> none  [on_device(): lax.psum_scatter(buffer.astype(jnp.bfloat16), 'dp', scatter_dimension=0,...]
    all_gather x1 -> x0, blocking collectives: 3.51 us -> none  [on_device(): gathered = lax.all_gather(update_rows[None], 'dp', axis=0, tiled=True)]
    unnamed x11 -> x7, local copies, waits for them, and re-layouts: 1.13 us -> 4.28 us
  transfers between devices with their start and end apart: 3 -> 0, of which waited for: 3 -> 0; matrix products, arithmetic and copies ran while one was open for 1% -> 0% of each run, Pallas kernels for 0% -> 0%
where the time goes in v1:
time: 69.5 us; the launch traced here: 69.4 us
  Pallas kernels  64.4 us (93%)
  local copies, waits for them, and re-layouts  4.28 us (6%)
    pallas_call x1, Pallas kernels, on_device(): pl.pallas_call(kernel, out_shape=[jax.ShapeDtypeStruct(stat_shape, F32),...  64.4 us
    unnamed x7, local copies, waits for them, and re-layouts  4.28 us

profile of v1, /device:TPU:1, one launch (start us, length us, event | category | flops | bytes accessed | tf_op | source)
XLA Modules:
  0.0 69.4 jit_solution(7165391557913943249)
XLA Ops:
  0.6 64.4 %shard_map.85 = (f32[6,2,16,1024]{3,2,1,0:T(8,128)}, f32[6,2,16,1024]{3,2,1,0:T(8,128)}, bf16[8,2,16,1024]{3,2,1,0:T(8,128)(2,1)}) custom-call(s32[8]{0:T(128)} %bitcast.17, bf16[8,2,16,1024]{3,2,1,0:T(8,128)(2,1)} %bitcast.14, f32[6,2,16,1024]{3,2,1,0:T(8,128)} %bitcast.11, f32[6,2,16,1024]{3,2,1,0:T(8,128)} %bitcast.12, bf16[6,2,16,1024]{3,2,1,0:T(8,128)(2,1)} %bitcast.15, ...), custom_call_target="tpu_custom_call" | custom-call | tf_op jit(solution)/shard_map/pallas_call | solution.py:319
  65.1 0.0 copy-start
  65.1 2.2 %copy.12 = f32[1,1,6,32,1024]{4,3,2,1,0:T(8,128)} copy(f32[1,1,6,32,1024]{4,3,2,1,0:T(8,128)} %bitcast.10) | data formatting | bytes 1572864
  67.2 0.0 copy-done
  67.2 0.0 copy-start.1
  67.2 0.9 %copy.13 = f32[1,1,6,32,1024]{4,3,2,1,0:T(8,128)} copy(f32[1,1,6,32,1024]{4,3,2,1,0:T(8,128)S(1)} %bitcast.9) | data formatting | bytes 1572864
  68.1 0.4 copy-done.1
  68.6 0.8 %copy.14 = bf16[8,32,1024]{2,1,0:T(8,128)(2,1)} copy(bf16[8,32,1024]{2,1,0:T(8,128)(2,1)S(1)} %bitcast.13) | data formatting | bytes 1048576
Async XLA Ops:
  65.1 2.2 %copy-start = (f32[6,2,16,1024]{3,2,1,0:T(8,128)S(1)}, f32[6,2,16,1024]{3,2,1,0:T(8,128)}, u32[]{:S(2)}) copy-start(f32[6,2,16,1024]{3,2,1,0:T(8,128)} %get-tuple-element.7) | copy-start | bytes 2359300
  67.2 1.3 %copy-start.1 = (bf16[8,2,16,1024]{3,2,1,0:T(8,128)(2,1)S(1)}, bf16[8,2,16,1024]{3,2,1,0:T(8,128)(2,1)}, u32[]{:S(2)}) copy-start(bf16[8,2,16,1024]{3,2,1,0:T(8,128)(2,1)} %get-tuple-element.8) | copy-start | bytes 1572868

commit v2 on v1

v2 whole, which is shorter than its diff:
```python
import functools
import math

import jax
import jax.numpy as jnp
from jax import lax
from jax.experimental import pallas as pl
from jax.experimental.pallas import tpu as pltpu
from jax.sharding import PartitionSpec as P

STAT_DECAY = 0.9
MESH = pl.DeviceIdType.MESH
NZ = 8
NY = 4
NX = 4
HALF = 16
WIDTH = 1024
KF = 8
SLOTS = 6
ORDER = (0, 1, 7, 2, 6, 3, 5, 4)
BATCHES = ((0, 1), (1, 4), (5, 3))
BF16 = jnp.bfloat16
F32 = jnp.float32


def kernel(
    owner_hbm, grad_ref, lstat_ref, rstat_ref, lroot_ref, rroot_ref,
    nleft_ref, nright_ref, upd_ref,
    owner_ref, own_g, got_g, part, lboth, rboth, lpart, rpart, lmine,
    gall, rall, scaled, lhs, lhs2, app, appk,
    norm_y, norm_x, norm_c, norm_z, norm_w,
    out_s, out_r0, out_r1, out_r2, lst, rst,
    loc_sem, c_rsem, z_rsem, gy_rsem, ry_rsem, gf_rsem, rf_rsem, n_rsem, o_rsem, fin_sem, s_sem,
):
    out_r = (out_r0, out_r1, out_r2)
    c = lax.axis_index("dp")
    x = lax.axis_index("fsdp")
    t = lax.axis_index("tensor")
    z, y = t // NY, t % NY
    oc = 1 - c

    def at_z(d):
        return {"tensor": lax.rem(z + d, NZ) * NY + y}

    def at_y(d):
        return {"tensor": z * NY + lax.rem(y + d, NY)}

    def at_x(d):
        return {"fsdp": lax.rem(x + d, NX)}

    def at_c(d):
        return {"dp": oc}

    def remote(src, dst, ssem, rsem, device):
        return pltpu.make_async_remote_copy(
            src_ref=src, dst_ref=dst, send_sem=s_sem.at[ssem], recv_sem=rsem,
            device_id=device, device_id_type=MESH,
        )

    def arrived(ref, rsem):
        remote(ref, ref, 0, rsem, at_c(1)).wait_recv()

    def departed(ref, ssem):
        remote(ref, ref, ssem, fin_sem.at[0], at_c(1)).wait_send()

    local = [
        pltpu.make_async_copy(grad_ref.at[:, c], own_g, loc_sem.at[0]),
        pltpu.make_async_copy(rroot_ref.at[:, c], rboth.at[c], loc_sem.at[1]),
        pltpu.make_async_copy(lroot_ref.at[:, c], lboth.at[c], loc_sem.at[2]),
        pltpu.make_async_copy(owner_hbm, owner_ref, loc_sem.at[3]),
        pltpu.make_async_copy(lstat_ref, lst, loc_sem.at[4]),
        pltpu.make_async_copy(rstat_ref, rst, loc_sem.at[5]),
    ]
    for copy in local[:4]:
        copy.start()

    peers = (
        [at_z(d) for d in range(1, NZ)]
        + [at_y(d) for d in range(1, NY)]
        + [at_x(d) for d in range(1, NX)]
        + [at_c(1)]
    )
    barrier = pltpu.get_barrier_semaphore()
    for peer in peers:
        pl.semaphore_signal(barrier, inc=1, device_id=peer, device_id_type=MESH)
    pl.semaphore_wait(barrier, len(peers))

    remote(grad_ref.at[:, oc], got_g, 0, c_rsem.at[0], at_c(1)).start()
    remote(rroot_ref.at[:, oc], rboth.at[c], 0, c_rsem.at[1], at_c(1)).start()
    remote(lroot_ref.at[:, oc], lboth.at[c], 0, c_rsem.at[2], at_c(1)).start()

    local[0].wait()
    arrived(got_g, c_rsem.at[0])

    def z_send(d, src, dst, rsem):
        remote(src.at[lax.rem(z + d, NZ)], dst, 1, rsem, at_z(d)).start()

    def y_send(d, ref, rsem):
        remote(ref, ref, 2, rsem, at_y(d)).start()

    def share(ref, rsem):
        remote(ref, ref, 3, rsem, at_c(1)).start()

    def batch(b):
        return pl.ds(*BATCHES[b])

    def from_y(d):
        return lax.rem(y + NY - d, NY)

    def pass_on(b):
        own = gall.at[batch(b), y, c]
        for d in (1, 3):
            y_send(d, own, gy_rsem.at[b, d])
        share(own, gf_rsem.at[0])

    squares = jnp.zeros((HALF, WIDTH), F32)
    for k, d in enumerate(ORDER):
        j = lax.rem(z + d, NZ)
        total = own_g[j].astype(F32) + got_g[j].astype(F32)
        squares += total * total
        if d:
            part[j] = total.astype(BF16)
            z_send(d, part, gall.at[k, y, c], z_rsem.at[0 if k < BATCHES[2][0] else 1])
        else:
            gall[0, y, c] = total.astype(BF16)
            pass_on(0)

    def norm_sends(k, buf, here, at, count):
        for d in range(1, count):
            remote(buf.at[here], buf.at[here], 4, n_rsem.at[k], at(d)).start()

    def norm_total(k, buf, count):
        arrived(buf.at[pl.ds(0, count - 1)], n_rsem.at[k])
        return jnp.sum(buf[...], axis=0)

    norm_y[y] = jnp.full((8, 128), jnp.sum(squares), F32)
    norm_sends(0, norm_y, y, at_y, NY)
    for copy in local[4:]:
        copy.start()

    local[3].wait()
    owners = [owner_ref[0, j] for j in range(KF)]
    ranks = []
    for j in range(KF):
        rank = jnp.int32(0)
        for i in range(j):
            rank += jnp.where(owners[i] == owners[j], 1, 0).astype(jnp.int32)
        ranks.append(jnp.minimum(rank, SLOTS - 1))

    local[1].wait()
    arrived(rboth.at[c], c_rsem.at[1])
    for j in range(KF):
        rpart[j] = rboth[owners[j], ranks[j]]
    local[2].wait()
    arrived(lboth.at[c], c_rsem.at[2])
    for j in range(KF):
        lpart[j] = lboth[owners[j], ranks[j]]
    rall[0, y, c] = rpart[z]
    lmine[z] = lpart[z]

    norm_x[x] = norm_total(0, norm_y, NY)
    norm_sends(1, norm_x, x, at_x, NX)

    row = lax.broadcasted_iota(jnp.int32, (128, WIDTH), 0)
    col = lax.broadcasted_iota(jnp.int32, (128, WIDTH), 1)
    pick = (row // HALF) * 128 + y * 32 + c * HALF + row % HALF
    lhs[pl.ds(128, 128), :] = jnp.where(col == pick, 1.0, 0.0).astype(BF16)

    def neighbours(b):
        for d in (1, 3):
            here = gall.at[batch(b), from_y(d), c]
            arrived(here, gy_rsem.at[b, d])
            if d == (1, 3)[b % 2]:
                y_send(d, here, gy_rsem.at[b, 2])
            share(here, gf_rsem.at[d])

    norm_c[c] = norm_total(1, norm_x, NX)
    norm_sends(2, norm_c, c, at_c, 2)
    norm_z[z] = norm_total(2, norm_c, 2)
    norm_sends(3, norm_z, z, at_z, NZ)
    neighbours(0)

    arrived(gall.at[batch(1), y, c], z_rsem.at[0])
    pass_on(1)
    arrived(gall.at[batch(2), y, c], z_rsem.at[1])
    pass_on(2)
    for k, d in enumerate(ORDER):
        if d:
            z_send(d, rpart, rall.at[k, y, c], z_rsem.at[2])
    for d in ORDER[1:]:
        z_send(d, lpart, lmine.at[z], z_rsem.at[3])

    clip = 2.0 * math.sqrt(NX * KF * WIDTH * WIDTH)
    norm = jnp.sqrt(norm_total(3, norm_z, NZ))
    factor = jnp.minimum(jnp.float32(1.0), clip / (norm + 1e-06))[0:1, 0:1]

    def scale(b, yy, cc):
        first, count = BATCHES[b]
        for k in range(first, first + count):
            zz = lax.rem(z + NZ - ORDER[k], NZ)
            scaled[zz, yy, cc] = (gall[k, yy, cc].astype(F32) * factor).astype(BF16)

    for b in range(3):
        scale(b, y, c)
    for d in (1, 3):
        scale(0, from_y(d), c)
    for b in (1, 2):
        neighbours(b)
        for d in (1, 3):
            scale(b, from_y(d), c)

    arrived(rall.at[pl.ds(1, NZ - 1), y, c], z_rsem.at[2])
    own = rall.at[:, y, c]
    for d in (1, 3, 2):
        y_send(d, own, ry_rsem.at[d])
    share(own, rf_rsem.at[0])

    for b in range(3):
        here = gall.at[batch(b), from_y(2), c]
        arrived(here, gy_rsem.at[b, 2])
        share(here, gf_rsem.at[2])
        scale(b, from_y(2), c)
    for d in (0, 1, 3, 2):
        arrived(gall.at[:, from_y(d), oc], gf_rsem.at[d])
        for b in range(3):
            scale(b, from_y(d), oc)
    lhs[pl.ds(0, 128), :] = scaled[:, y, c].reshape(128, WIDTH)

    def o_sends(k):
        for d in ORDER[1:]:
            z_send(d, out_s.at[k], out_r[k].at[z, c], z_rsem.at[4 + k])
        out_r[k][z, c] = out_s[k, z]

    nt = (((1,), (1,)), ((), ()))
    for n in range(4):
        g_rows = scaled[pl.ds(2 * n, 2)].reshape(256, WIDTH)
        both = lax.dot_general(lhs[...], g_rows, nt, preferred_element_type=F32).astype(BF16)
        out_s[0, :, :, pl.ds(256 * n, 256)] = both[:128].reshape(NZ, HALF, 256)
        lhs2[pl.ds(0, 128), pl.ds(256 * n, 256)] = both[128:]
    o_sends(0)
    arrived(lmine.at[pl.ds(0, NZ - 1)], z_rsem.at[3])
    lhs2[pl.ds(128, 128), :] = lmine[...].reshape(128, WIDTH)
    for n in range(4):
        g_cols = scaled[:, :, :, :, pl.ds(256 * n, 256)].reshape(WIDTH, 256)
        both = jnp.dot(lhs2[...], g_cols, preferred_element_type=F32).astype(BF16)
        out_s[1, :, :, pl.ds(256 * n, 256)] = both[:128].reshape(NZ, HALF, 256)
        app[:, pl.ds(256 * n, 256)] = both[128:]
    o_sends(1)

    for k, d in enumerate(ORDER):
        from_z = pl.multiple_of(lax.rem(z + NZ - d, NZ) * 128, 128)
        appk[:, pl.ds(128 * k, 128)] = app[:, pl.ds(from_z, 128)]
    for d in (1, 3, 2):
        here = rall.at[:, from_y(d), c]
        arrived(here, ry_rsem.at[d])
        share(here, rf_rsem.at[0])
    arrived(rall.at[:, :, oc], rf_rsem.at[0])
    for n in range(4):
        r_cols = rall[:, :, :, :, pl.ds(256 * n, 256)].reshape(WIDTH, 256)
        upd = jnp.dot(appk[...], r_cols, preferred_element_type=F32).astype(BF16)
        out_s[2, :, :, pl.ds(256 * n, 256)] = upd.reshape(NZ, HALF, 256)
    o_sends(2)

    places, taken = [], []
    for s in range(SLOTS):
        place, count = jnp.int32(0), jnp.int32(0)
        for j in range(KF):
            hit = (owners[j] == c) & (ranks[j] == s)
            place = jnp.where(hit, j, place)
            count = jnp.where(hit, 1, count)
        places.append(place)
        taken.append(count)

    mix = (1.0 - STAT_DECAY) / WIDTH

    def finish(k):
        arrived(out_r[k].at[pl.ds(0, NZ - 1), c], z_rsem.at[4 + k])
        here = out_r[k].at[:, c]
        remote(here, here, 5, o_rsem.at[k], at_c(1)).start()
        arrived(out_r[k].at[:, oc], o_rsem.at[k])

    def stats(k, buf, out_ref):
        for s in range(SLOTS):
            gram = out_r[k][places[s]].astype(F32)
            new = STAT_DECAY * buf[s] + mix * gram
            buf[s] = jnp.where(taken[s] > 0, new, buf[s])
        copy = pltpu.make_async_copy(buf, out_ref, fin_sem.at[k])
        copy.start()
        return copy

    local[4].wait()
    finish(0)
    done_left = stats(0, lst, nleft_ref)
    local[5].wait()
    finish(1)
    done_right = stats(1, rst, nright_ref)
    finish(2)
    done_upd = pltpu.make_async_copy(out_r2, upd_ref, fin_sem.at[2])
    done_upd.start()

    departed(gall.at[pl.ds(0, 5), :, 0], 0)
    departed(gall.at[pl.ds(0, 7), pl.ds(0, 3)], 1)
    departed(gall.at[pl.ds(0, 6)], 2)
    departed(gall, 3)
    departed(norm_w, 4)
    departed(gall.at[pl.ds(0, 3)], 5)
    for copy in (done_left, done_right, done_upd):
        copy.wait()


def on_device(gradients, owner_lists, left_stats, right_stats, left_roots, right_roots):
    any_space = pl.BlockSpec(memory_space=pl.ANY)
    vmem, dma = pltpu.VMEM, pltpu.SemaphoreType.DMA
    stat_shape = (SLOTS, 2, HALF, WIDTH)
    new_left, new_right, updates = pl.pallas_call(
        kernel,
        out_shape=[
            jax.ShapeDtypeStruct(stat_shape, F32),
            jax.ShapeDtypeStruct(stat_shape, F32),
            jax.ShapeDtypeStruct((KF, 2, HALF, WIDTH), BF16),
        ],
        in_specs=[any_space] * 6,
        out_specs=[any_space] * 3,
        scratch_shapes=[
            pltpu.SMEM((1, KF), jnp.int32),
            vmem((KF, HALF, WIDTH), BF16),
            vmem((KF, HALF, WIDTH), BF16),
            vmem((KF, HALF, WIDTH), BF16),
            vmem((2, SLOTS, HALF, WIDTH), BF16),
            vmem((2, SLOTS, HALF, WIDTH), BF16),
            vmem((KF, HALF, WIDTH), BF16),
            vmem((KF, HALF, WIDTH), BF16),
            vmem((NZ, HALF, WIDTH), BF16),
            vmem((NZ, NY, 2, HALF, WIDTH), BF16),
            vmem((NZ, NY, 2, HALF, WIDTH), BF16),
            vmem((NZ, NY, 2, HALF, WIDTH), BF16),
            vmem((256, WIDTH), BF16),
            vmem((256, WIDTH), BF16),
            vmem((128, WIDTH), BF16),
            vmem((128, WIDTH), BF16),
            vmem((NY, 8, 128), F32),
            vmem((NX, 8, 128), F32),
            vmem((2, 8, 128), F32),
            vmem((NZ, 8, 128), F32),
            vmem((14, 8, 128), F32),
            vmem((3, NZ, HALF, WIDTH), BF16),
            vmem((KF, 2, HALF, WIDTH), BF16),
            vmem((KF, 2, HALF, WIDTH), BF16),
            vmem((KF, 2, HALF, WIDTH), BF16),
            vmem(stat_shape, F32),
            vmem(stat_shape, F32),
            dma((6,)),
            dma((3,)),
            dma((7,)),
            dma((3, NY)),
            dma((NY,)),
            dma((NY,)),
            dma((1,)),
            dma((4,)),
            dma((3,)),
            dma((3,)),
            dma((6,)),
        ],
        compiler_params=pltpu.CompilerParams(
            collective_id=0, has_side_effects=True, vmem_limit_bytes=60 * 2**20
        ),
    )(
        owner_lists,
        gradients.reshape(KF, 2, HALF, WIDTH),
        left_stats.reshape(stat_shape),
        right_stats.reshape(stat_shape),
        left_roots.reshape(stat_shape),
        right_roots.reshape(stat_shape),
    )
    full = (1, 1, SLOTS, 2 * HALF, WIDTH)
    return (
        new_left.reshape(full),
        new_right.reshape(full),
        updates.reshape(KF, 2 * HALF, WIDTH),
    )


def solution(mesh):
    placed = (
        P("dp", "fsdp", "tensor", None),
        P("fsdp", None),
        P("dp", "fsdp", None, "tensor", None),
        P("dp", "fsdp", None, "tensor", None),
        P("dp", "fsdp", None, "tensor", None),
        P("dp", "fsdp", None, "tensor", None),
    )
    return jax.shard_map(
        on_device,
        mesh=mesh,
        in_specs=placed,
        out_specs=(
            P("dp", "fsdp", None, "tensor", None),
            P("dp", "fsdp", None, "tensor", None),
            P("fsdp", "tensor", None),
        ),
        check_vma=False,
    )
```

time: 69.5 us -> 61.1 us (0.88)
  Pallas kernels: 64.4 us -> 56 us
    pallas_call x1, Pallas kernels: 64.4 us -> 56 us  [on_device(): pl.pallas_call(kernel, out_shape=[jax.ShapeDtypeStruct(stat_shape, F32),...]
where the time goes in v2:
time: 61.1 us; the launch traced here: 60.9 us
  Pallas kernels  56 us (92%)
  local copies, waits for them, and re-layouts  4.28 us (7%)
  between operations  0.65 us (1%)
    pallas_call x1, Pallas kernels, on_device(): pl.pallas_call(kernel, out_shape=[jax.ShapeDtypeStruct(stat_shape, F32),...  56 us
    unnamed x7, local copies, waits for them, and re-layouts  4.28 us

profile of v2, /device:TPU:1, one launch (start us, length us, event | category | flops | bytes accessed | tf_op | source)
XLA Modules:
  0.0 60.9 jit_solution(7802175221094285726)
XLA Ops:
  0.6 56.0 %shard_map.85 = (f32[6,2,16,1024]{3,2,1,0:T(8,128)}, f32[6,2,16,1024]{3,2,1,0:T(8,128)}, bf16[8,2,16,1024]{3,2,1,0:T(8,128)(2,1)}) custom-call(s32[1,8]{1,0:T(1,128)} %owner_hbm.1, bf16[8,2,16,1024]{3,2,1,0:T(8,128)(2,1)} %bitcast.13, f32[6,2,16,1024]{3,2,1,0:T(8,128)} %bitcast.10, f32[6,2,16,1024]{3,2,1,0:T(8,128)} %bitcast.11, ...), custom_call_target="tpu_custom_call" | custom-call | tf_op jit(solution)/shard_map/pallas_call | solution.py:315
  56.6 0.0 copy-start
  56.6 2.2 %copy.12 = f32[1,1,6,32,1024]{4,3,2,1,0:T(8,128)} copy(f32[1,1,6,32,1024]{4,3,2,1,0:T(8,128)} %bitcast.9) | data formatting | bytes 1572864
  58.8 0.0 copy-done
  58.8 0.0 copy-start.1
  58.8 0.9 %copy.13 = f32[1,1,6,32,1024]{4,3,2,1,0:T(8,128)} copy(f32[1,1,6,32,1024]{4,3,2,1,0:T(8,128)S(1)} %bitcast.8) | data formatting | bytes 1572864
  59.6 0.4 copy-done.1
  60.1 0.8 %copy.14 = bf16[8,32,1024]{2,1,0:T(8,128)(2,1)} copy(bf16[8,32,1024]{2,1,0:T(8,128)(2,1)S(1)} %bitcast.12) | data formatting | bytes 1048576
Async XLA Ops:
  56.6 2.2 %copy-start = (f32[6,2,16,1024]{3,2,1,0:T(8,128)S(1)}, f32[6,2,16,1024]{3,2,1,0:T(8,128)}, u32[]{:S(2)}) copy-start(f32[6,2,16,1024]{3,2,1,0:T(8,128)} %get-tuple-element.7) | copy-start | bytes 2359300
  58.8 1.3 %copy-start.1 = (bf16[8,2,16,1024]{3,2,1,0:T(8,128)(2,1)S(1)}, bf16[8,2,16,1024]{3,2,1,0:T(8,128)(2,1)}, u32[]{:S(2)}) copy-start(bf16[8,2,16,1024]{3,2,1,0:T(8,128)(2,1)} %get-tuple-element.8) | copy-start | bytes 1572868

commit v3 on v2

--- a/solution.py
+++ b/solution.py
@@ -15,10 +15,12 @@
 NX = 4
 HALF = 16
 WIDTH = 1024
+LANES = 128
+WEDGE = 5
 KF = 8
 SLOTS = 6
 ORDER = (0, 1, 7, 2, 6, 3, 5, 4)
-BATCHES = ((0, 1), (1, 4), (5, 3))
+BATCHES = ((0, 1), (1, 2), (3, 2), (5, 2), (7, 1))
 BF16 = jnp.bfloat16
 F32 = jnp.float32
 
@@ -27,7 +29,7 @@
     owner_hbm, grad_ref, lstat_ref, rstat_ref, lroot_ref, rroot_ref,
     nleft_ref, nright_ref, upd_ref,
     owner_ref, own_g, got_g, part, lboth, rboth, lpart, rpart, lmine,
-    gall, rall, scaled, lhs, lhs2, app, appk,
+    gall, rh, scaled, rfull, lhs, lhs2, app,
     norm_y, norm_x, norm_c, norm_z, norm_w,
     out_s, out_r0, out_r1, out_r2, lst, rst,
     loc_sem, c_rsem, z_rsem, gy_rsem, ry_rsem, gf_rsem, rf_rsem, n_rsem, o_rsem, fin_sem, s_sem,
@@ -92,14 +94,14 @@
     local[0].wait()
     arrived(got_g, c_rsem.at[0])
 
-    def z_send(d, src, dst, rsem):
-        remote(src.at[lax.rem(z + d, NZ)], dst, 1, rsem, at_z(d)).start()
-
-    def y_send(d, ref, rsem):
-        remote(ref, ref, 2, rsem, at_y(d)).start()
-
-    def share(ref, rsem):
-        remote(ref, ref, 3, rsem, at_c(1)).start()
+    def z_send(d, src, dst, rsem, ssem=1):
+        remote(src.at[lax.rem(z + d, NZ)], dst, ssem, rsem, at_z(d)).start()
+
+    def y_send(d, ref, rsem, ssem=2):
+        remote(ref, ref, ssem, rsem, at_y(d)).start()
+
+    def share(ref, rsem, ssem=3):
+        remote(ref, ref, ssem, rsem, at_c(1)).start()
 
     def batch(b):
         return pl.ds(*BATCHES[b])
@@ -109,9 +111,14 @@
 
     def pass_on(b):
         own = gall.at[batch(b), y, c]
-        for d in (1, 3):
+        for d in (1, 3, 2):
             y_send(d, own, gy_rsem.at[b, d])
         share(own, gf_rsem.at[0])
+
+    def wave(b):
+        first, count = BATCHES[b]
+        for k in range(first, first + count):
+            z_send(ORDER[k], part, gall.at[k, y, c], z_rsem.at[b - 1])
 
     squares = jnp.zeros((HALF, WIDTH), F32)
     for k, d in enumerate(ORDER):
@@ -120,10 +127,12 @@
         squares += total * total
         if d:
             part[j] = total.astype(BF16)
-            z_send(d, part, gall.at[k, y, c], z_rsem.at[0 if k < BATCHES[2][0] else 1])
         else:
             gall[0, y, c] = total.astype(BF16)
-            pass_on(0)
+        if k == 2:
+            wave(1)
+        if k == 4:
+            wave(2)
 
     def norm_sends(k, buf, here, at, count):
         for d in range(1, count):
@@ -135,6 +144,7 @@
 
     norm_y[y] = jnp.full((8, 128), jnp.sum(squares), F32)
     norm_sends(0, norm_y, y, at_y, NY)
+    pass_on(0)
     for copy in local[4:]:
         copy.start()
 
@@ -147,48 +157,65 @@
             rank += jnp.where(owners[i] == owners[j], 1, 0).astype(jnp.int32)
         ranks.append(jnp.minimum(rank, SLOTS - 1))
 
+    def wedge(both, parts, half):
+        for j in range(KF):
+            for m in range(WEDGE):
+                there = pl.multiple_of(lax.rem(z + m, NZ) * LANES, LANES)
+                parts[j, :, pl.ds(LANES * m, LANES)] = both[
+                    owners[j], ranks[j], :, pl.ds(there, LANES)
+                ]
+        half[0, y, c] = parts[z]
+
+    def wedge_sends(parts, half, rsem):
+        for d in ORDER[1:]:
+            z_send(d, parts, half.at[NZ - d, y, c], rsem, 6)
+
+    def unfold(half, full):
+        for k in range(NZ):
+            zz = lax.rem(z + k, NZ)
+            here = pl.multiple_of(zz * LANES, LANES)
+            for m in range(WEDGE):
+                tile = half[k, :, :, :, pl.ds(LANES * m, LANES)]
+                ww = lax.rem(z + k + m, NZ)
+                there = pl.multiple_of(ww * LANES, LANES)
+                full[zz, :, :, :, pl.ds(there, LANES)] = tile
+                if m in (1, 2, 3):
+                    turned = tile.reshape(LANES, LANES).T
+                    full[ww, :, :, :, pl.ds(here, LANES)] = turned.reshape(NY, 2, HALF, LANES)
+
     local[1].wait()
     arrived(rboth.at[c], c_rsem.at[1])
-    for j in range(KF):
-        rpart[j] = rboth[owners[j], ranks[j]]
+    wedge(rboth, rpart, rh)
     local[2].wait()
     arrived(lboth.at[c], c_rsem.at[2])
     for j in range(KF):
         lpart[j] = lboth[owners[j], ranks[j]]
-    rall[0, y, c] = rpart[z]
     lmine[z] = lpart[z]
 
+    arrived(gall.at[batch(1), y, c], z_rsem.at[0])
+    wave(3)
+    pass_on(1)
     norm_x[x] = norm_total(0, norm_y, NY)
     norm_sends(1, norm_x, x, at_x, NX)
+    arrived(gall.at[batch(2), y, c], z_rsem.at[1])
+    wave(4)
+    pass_on(2)
+    norm_c[c] = norm_total(1, norm_x, NX)
+    norm_sends(2, norm_c, c, at_c, 2)
+    norm_z[z] = norm_total(2, norm_c, 2)
+    norm_sends(3, norm_z, z, at_z, NZ)
+    arrived(gall.at[batch(3), y, c], z_rsem.at[2])
+    wedge_sends(rpart, rh, z_rsem.at[4])
+    pass_on(3)
+    arrived(gall.at[batch(4), y, c], z_rsem.at[3])
+    pass_on(4)
+    for d in ORDER[1:]:
+        z_send(d, lpart, lmine.at[z], z_rsem.at[5], 9)
 
     row = lax.broadcasted_iota(jnp.int32, (128, WIDTH), 0)
     col = lax.broadcasted_iota(jnp.int32, (128, WIDTH), 1)
     pick = (row // HALF) * 128 + y * 32 + c * HALF + row % HALF
     lhs[pl.ds(128, 128), :] = jnp.where(col == pick, 1.0, 0.0).astype(BF16)
-
-    def neighbours(b):
-        for d in (1, 3):
-            here = gall.at[batch(b), from_y(d), c]
-            arrived(here, gy_rsem.at[b, d])
-            if d == (1, 3)[b % 2]:
-                y_send(d, here, gy_rsem.at[b, 2])
-            share(here, gf_rsem.at[d])
-
-    norm_c[c] = norm_total(1, norm_x, NX)
-    norm_sends(2, norm_c, c, at_c, 2)
-    norm_z[z] = norm_total(2, norm_c, 2)
-    norm_sends(3, norm_z, z, at_z, NZ)
-    neighbours(0)
-
-    arrived(gall.at[batch(1), y, c], z_rsem.at[0])
-    pass_on(1)
-    arrived(gall.at[batch(2), y, c], z_rsem.at[1])
-    pass_on(2)
-    for k, d in enumerate(ORDER):
-        if d:
-            z_send(d, rpart, rall.at[k, y, c], z_rsem.at[2])
-    for d in ORDER[1:]:
-        z_send(d, lpart, lmine.at[z], z_rsem.at[3])
 
     clip = 2.0 * math.sqrt(NX * KF * WIDTH * WIDTH)
     norm = jnp.sqrt(norm_total(3, norm_z, NZ))
@@ -200,35 +227,41 @@
             zz = lax.rem(z + NZ - ORDER[k], NZ)
             scaled[zz, yy, cc] = (gall[k, yy, cc].astype(F32) * factor).astype(BF16)
 
-    for b in range(3):
+    for b in range(5):
         scale(b, y, c)
-    for d in (1, 3):
-        scale(0, from_y(d), c)
-    for b in (1, 2):
-        neighbours(b)
-        for d in (1, 3):
+    for b in range(5):
+        for d in (1, 3, 2):
+            here = gall.at[batch(b), from_y(d), c]
+            arrived(here, gy_rsem.at[b, d])
+            share(here, gf_rsem.at[d])
+        for d in (1, 3, 2):
             scale(b, from_y(d), c)
 
-    arrived(rall.at[pl.ds(1, NZ - 1), y, c], z_rsem.at[2])
-    own = rall.at[:, y, c]
-    for d in (1, 3, 2):
-        y_send(d, own, ry_rsem.at[d])
-    share(own, rf_rsem.at[0])
-
-    for b in range(3):
-        here = gall.at[batch(b), from_y(2), c]
-        arrived(here, gy_rsem.at[b, 2])
-        share(here, gf_rsem.at[2])
-        scale(b, from_y(2), c)
+    def pass_roots(i, half):
+        own = half.at[:, y, c]
+        arrived(half.at[pl.ds(1, NZ - 1), y, c], z_rsem.at[4 + i])
+        for d in (1, 3, 2):
+            y_send(d, own, ry_rsem.at[i, d], 7)
+        share(own, rf_rsem.at[i], 8)
+
+    def gathered(i, half):
+        for d in (1, 3, 2):
+            here = half.at[:, from_y(d), c]
+            arrived(here, ry_rsem.at[i, d])
+            share(here, rf_rsem.at[i], 8)
+        arrived(half.at[:, :, oc], rf_rsem.at[i])
+
+    pass_roots(0, rh)
+
     for d in (0, 1, 3, 2):
         arrived(gall.at[:, from_y(d), oc], gf_rsem.at[d])
-        for b in range(3):
+        for b in range(5):
             scale(b, from_y(d), oc)
     lhs[pl.ds(0, 128), :] = scaled[:, y, c].reshape(128, WIDTH)
 
     def o_sends(k):
         for d in ORDER[1:]:
-            z_send(d, out_s.at[k], out_r[k].at[z, c], z_rsem.at[4 + k])
+            z_send(d, out_s.at[k], out_r[k].at[z, c], z_rsem.at[6 + k])
         out_r[k][z, c] = out_s[k, z]
 
     nt = (((1,), (1,)), ((), ()))
@@ -236,28 +269,25 @@
         g_rows = scaled[pl.ds(2 * n, 2)].reshape(256, WIDTH)
         both = lax.dot_general(lhs[...], g_rows, nt, preferred_element_type=F32).astype(BF16)
         out_s[0, :, :, pl.ds(256 * n, 256)] = both[:128].reshape(NZ, HALF, 256)
-        lhs2[pl.ds(0, 128), pl.ds(256 * n, 256)] = both[128:]
+        lhs2[:, pl.ds(256 * n, 256)] = both[128:]
     o_sends(0)
-    arrived(lmine.at[pl.ds(0, NZ - 1)], z_rsem.at[3])
-    lhs2[pl.ds(128, 128), :] = lmine[...].reshape(128, WIDTH)
     for n in range(4):
         g_cols = scaled[:, :, :, :, pl.ds(256 * n, 256)].reshape(WIDTH, 256)
         both = jnp.dot(lhs2[...], g_cols, preferred_element_type=F32).astype(BF16)
-        out_s[1, :, :, pl.ds(256 * n, 256)] = both[:128].reshape(NZ, HALF, 256)
-        app[:, pl.ds(256 * n, 256)] = both[128:]
+        out_s[1, :, :, pl.ds(256 * n, 256)] = both.reshape(NZ, HALF, 256)
     o_sends(1)
-
-    for k, d in enumerate(ORDER):
-        from_z = pl.multiple_of(lax.rem(z + NZ - d, NZ) * 128, 128)
-        appk[:, pl.ds(128 * k, 128)] = app[:, pl.ds(from_z, 128)]
-    for d in (1, 3, 2):
-        here = rall.at[:, from_y(d), c]
-        arrived(here, ry_rsem.at[d])
-        share(here, rf_rsem.at[0])
-    arrived(rall.at[:, :, oc], rf_rsem.at[0])
+    gathered(0, rh)
+    unfold(rh, rfull)
+    arrived(lmine.at[pl.ds(0, NZ - 1)], z_rsem.at[5])
+    left = lmine[...].reshape(128, WIDTH)
     for n in range(4):
-        r_cols = rall[:, :, :, :, pl.ds(256 * n, 256)].reshape(WIDTH, 256)
-        upd = jnp.dot(appk[...], r_cols, preferred_element_type=F32).astype(BF16)
+        g_cols = scaled[:, :, :, :, pl.ds(256 * n, 256)].reshape(WIDTH, 256)
+        app[:, pl.ds(256 * n, 256)] = jnp.dot(
+            left, g_cols, preferred_element_type=F32
+        ).astype(BF16)
+    for n in range(4):
+        r_cols = rfull[:, :, :, :, pl.ds(256 * n, 256)].reshape(WIDTH, 256)
+        upd = jnp.dot(app[...], r_cols, preferred_element_type=F32).astype(BF16)
         out_s[2, :, :, pl.ds(256 * n, 256)] = upd.reshape(NZ, HALF, 256)
     o_sends(2)
 
@@ -274,7 +304,7 @@
     mix = (1.0 - STAT_DECAY) / WIDTH
 
     def finish(k):
-        arrived(out_r[k].at[pl.ds(0, NZ - 1), c], z_rsem.at[4 + k])
+        arrived(out_r[k].at[pl.ds(0, NZ - 1), c], z_rsem.at[6 + k])
         here = out_r[k].at[:, c]
         remote(here, here, 5, o_rsem.at[k], at_c(1)).start()
         arrived(out_r[k].at[:, oc], o_rsem.at[k])
@@ -294,14 +324,20 @@
     local[5].wait()
     finish(1)
     done_right = stats(1, rst, nright_ref)
-    finish(2)
-    done_upd = pltpu.make_async_copy(out_r2, upd_ref, fin_sem.at[2])
+    arrived(out_r2.at[pl.ds(0, NZ - 1), c], z_rsem.at[8])
+    done_upd = pltpu.make_async_copy(out_r2.at[:, c], upd_ref.at[:, c], fin_sem.at[2])
     done_upd.start()
+    remote(out_r2.at[:, c], upd_ref.at[:, c], 5, o_rsem.at[2], at_c(1)).start()
+    arrived(upd_ref.at[:, oc], o_rsem.at[2])
 
     departed(gall.at[pl.ds(0, 5), :, 0], 0)
-    departed(gall.at[pl.ds(0, 7), pl.ds(0, 3)], 1)
-    departed(gall.at[pl.ds(0, 6)], 2)
-    departed(gall, 3)
+    departed(gall.at[pl.ds(0, 7), pl.ds(0, 2)], 1)
+    departed(lpart.at[pl.ds(0, 7)], 9)
+    departed(gall.at[pl.ds(0, 3)], 2)
+    departed(gall.at[pl.ds(0, 4)], 3)
+    departed(rpart.at[pl.ds(0, 7)], 6)
+    departed(rh.at[pl.ds(0, 3)], 7)
+    departed(rh.at[pl.ds(0, 4)], 8)
     departed(norm_w, 4)
     departed(gall.at[pl.ds(0, 3)], 5)
     for copy in (done_left, done_right, done_upd):
@@ -329,12 +365,12 @@
             vmem((2, SLOTS, HALF, WIDTH), BF16),
             vmem((2, SLOTS, HALF, WIDTH), BF16),
             vmem((KF, HALF, WIDTH), BF16),
-            vmem((KF, HALF, WIDTH), BF16),
+            vmem((KF, HALF, WEDGE * LANES), BF16),
             vmem((NZ, HALF, WIDTH), BF16),
             vmem((NZ, NY, 2, HALF, WIDTH), BF16),
+            vmem((NZ, NY, 2, HALF, WEDGE * LANES), BF16),
             vmem((NZ, NY, 2, HALF, WIDTH), BF16),
             vmem((NZ, NY, 2, HALF, WIDTH), BF16),
-            vmem((256, WIDTH), BF16),
             vmem((256, WIDTH), BF16),
             vmem((128, WIDTH), BF16),
             vmem((128, WIDTH), BF16),
@@ -351,15 +387,15 @@
             vmem(stat_shape, F32),
             dma((6,)),
             dma((3,)),
-            dma((7,)),
-            dma((3, NY)),
-            dma((NY,)),
+            dma((9,)),
+            dma((5, NY)),
+            dma((1, NY)),
             dma((NY,)),
             dma((1,)),
             dma((4,)),
             dma((3,)),
             dma((3,)),
-            dma((6,)),
+            dma((10,)),
         ],
         compiler_params=pltpu.CompilerParams(
             collective_id=0, has_side_effects=True, vmem_limit_bytes=60 * 2**20

time: 61.1 us -> 56.3 us (0.921)
  Pallas kernels: 56 us -> 50.8 us
    pallas_call x1, Pallas kernels: 56 us -> 50.8 us  [on_device(): pl.pallas_call(kernel, out_shape=[jax.ShapeDtypeStruct(stat_shape, F32),...]
where the time goes in v3:
time: 56.3 us; the launch traced here: 55.7 us
  Pallas kernels  50.8 us (90%)
  local copies, waits for them, and re-layouts  4.28 us (8%)
  between operations  0.65 us (1%)
    pallas_call x1, Pallas kernels, on_device(): pl.pallas_call(kernel, out_shape=[jax.ShapeDtypeStruct(stat_shape, F32),...  50.8 us
    unnamed x7, local copies, waits for them, and re-layouts  4.28 us

profile of v3, /device:TPU:1, one launch (start us, length us, event | category | flops | bytes accessed | tf_op | source)
XLA Modules:
  0.0 55.7 jit_solution(7264973225818163247)
XLA Ops:
  0.6 50.8 %shard_map.85 = (f32[6,2,16,1024]{3,2,1,0:T(8,128)}, f32[6,2,16,1024]{3,2,1,0:T(8,128)}, bf16[8,2,16,1024]{3,2,1,0:T(8,128)(2,1)}) custom-call(s32[1,8]{1,0:T(1,128)} %owner_hbm.1, bf16[8,2,16,1024]{3,2,1,0:T(8,128)(2,1)} %bitcast.13, f32[6,2,16,1024]{3,2,1,0:T(8,128)} %bitcast.10, f32[6,2,16,1024]{3,2,1,0:T(8,128)} %bitcast.11, ...), custom_call_target="tpu_custom_call" | custom-call | tf_op jit(solution)/shard_map/pallas_call | solution.py:351
  51.4 0.0 copy-start
  51.5 2.2 %copy.12 = f32[1,1,6,32,1024]{4,3,2,1,0:T(8,128)} copy(f32[1,1,6,32,1024]{4,3,2,1,0:T(8,128)} %bitcast.9) | data formatting | bytes 1572864
  53.6 0.0 copy-done
  53.6 0.0 copy-start.1
  53.6 0.9 %copy.13 = f32[1,1,6,32,1024]{4,3,2,1,0:T(8,128)} copy(f32[1,1,6,32,1024]{4,3,2,1,0:T(8,128)S(1)} %bitcast.8) | data formatting | bytes 1572864
  54.5 0.4 copy-done.1
  54.9 0.8 %copy.14 = bf16[8,32,1024]{2,1,0:T(8,128)(2,1)} copy(bf16[8,32,1024]{2,1,0:T(8,128)(2,1)S(1)} %bitcast.12) | data formatting | bytes 1048576
Async XLA Ops:
  51.4 2.2 %copy-start = (f32[6,2,16,1024]{3,2,1,0:T(8,128)S(1)}, f32[6,2,16,1024]{3,2,1,0:T(8,128)}, u32[]{:S(2)}) copy-start(f32[6,2,16,1024]{3,2,1,0:T(8,128)} %get-tuple-element.7) | copy-start | bytes 2359300
  53.6 1.3 %copy-start.1 = (bf16[8,2,16,1024]{3,2,1,0:T(8,128)(2,1)S(1)}, bf16[8,2,16,1024]{3,2,1,0:T(8,128)(2,1)}, u32[]{:S(2)}) copy-start(bf16[8,2,16,1024]{3,2,1,0:T(8,128)(2,1)} %get-tuple-element.8) | copy-start | bytes 1572868

commit v4 on v3

--- a/solution.py
+++ b/solution.py
@@ -29,7 +29,7 @@
     owner_hbm, grad_ref, lstat_ref, rstat_ref, lroot_ref, rroot_ref,
     nleft_ref, nright_ref, upd_ref,
     owner_ref, own_g, got_g, part, lboth, rboth, lpart, rpart, lmine,
-    gall, rh, scaled, rfull, lhs, lhs2, app,
+    gall, rh, scaled, rfull, lhs, lhs2, left, app,
     norm_y, norm_x, norm_c, norm_z, norm_w,
     out_s, out_r0, out_r1, out_r2, lst, rst,
     loc_sem, c_rsem, z_rsem, gy_rsem, ry_rsem, gf_rsem, rf_rsem, n_rsem, o_rsem, fin_sem, s_sem,
@@ -113,7 +113,7 @@
         own = gall.at[batch(b), y, c]
         for d in (1, 3, 2):
             y_send(d, own, gy_rsem.at[b, d])
-        share(own, gf_rsem.at[0])
+        share(own, gf_rsem.at[b])
 
     def wave(b):
         first, count = BATCHES[b]
@@ -131,8 +131,6 @@
             gall[0, y, c] = total.astype(BF16)
         if k == 2:
             wave(1)
-        if k == 4:
-            wave(2)
 
     def norm_sends(k, buf, here, at, count):
         for d in range(1, count):
@@ -166,8 +164,8 @@
                 ]
         half[0, y, c] = parts[z]
 
-    def wedge_sends(parts, half, rsem):
-        for d in ORDER[1:]:
+    def wedge_sends(parts, half, rsem, order=ORDER[1:]):
+        for d in order:
             z_send(d, parts, half.at[NZ - d, y, c], rsem, 6)
 
     def unfold(half, full):
@@ -192,20 +190,21 @@
         lpart[j] = lboth[owners[j], ranks[j]]
     lmine[z] = lpart[z]
 
+    wave(2)
+    wave(3)
     arrived(gall.at[batch(1), y, c], z_rsem.at[0])
-    wave(3)
     pass_on(1)
     norm_x[x] = norm_total(0, norm_y, NY)
     norm_sends(1, norm_x, x, at_x, NX)
+    wave(4)
     arrived(gall.at[batch(2), y, c], z_rsem.at[1])
-    wave(4)
     pass_on(2)
     norm_c[c] = norm_total(1, norm_x, NX)
     norm_sends(2, norm_c, c, at_c, 2)
     norm_z[z] = norm_total(2, norm_c, 2)
     norm_sends(3, norm_z, z, at_z, NZ)
+    wedge_sends(rpart, rh, z_rsem.at[4])
     arrived(gall.at[batch(3), y, c], z_rsem.at[2])
-    wedge_sends(rpart, rh, z_rsem.at[4])
     pass_on(3)
     arrived(gall.at[batch(4), y, c], z_rsem.at[3])
     pass_on(4)
@@ -215,27 +214,40 @@
     row = lax.broadcasted_iota(jnp.int32, (128, WIDTH), 0)
     col = lax.broadcasted_iota(jnp.int32, (128, WIDTH), 1)
     pick = (row // HALF) * 128 + y * 32 + c * HALF + row % HALF
-    lhs[pl.ds(128, 128), :] = jnp.where(col == pick, 1.0, 0.0).astype(BF16)
+    one_hot = jnp.where(col == pick, 1.0, 0.0).astype(BF16)
+    lhs[pl.ds(NZ, NZ)] = one_hot.reshape(NZ, HALF, WIDTH)
 
     clip = 2.0 * math.sqrt(NX * KF * WIDTH * WIDTH)
     norm = jnp.sqrt(norm_total(3, norm_z, NZ))
     factor = jnp.minimum(jnp.float32(1.0), clip / (norm + 1e-06))[0:1, 0:1]
 
-    def scale(b, yy, cc):
+    def times(ref):
+        return (ref[...].astype(F32) * factor).astype(BF16)
+
+    def column(k):
+        return pl.multiple_of(lax.rem(z + NZ - ORDER[k], NZ) * LANES, LANES)
+
+    for k in range(NZ):
+        lhs[lax.rem(z + NZ - ORDER[k], NZ)] = times(gall.at[k, y, c])
+
+    nt = (((1,), (1,)), ((), ()))
+
+    def whole(b):
+        arrived(gall.at[batch(b), :, oc], gf_rsem.at[b])
         first, count = BATCHES[b]
         for k in range(first, first + count):
-            zz = lax.rem(z + NZ - ORDER[k], NZ)
-            scaled[zz, yy, cc] = (gall[k, yy, cc].astype(F32) * factor).astype(BF16)
-
-    for b in range(5):
-        scale(b, y, c)
-    for b in range(5):
-        for d in (1, 3, 2):
-            here = gall.at[batch(b), from_y(d), c]
-            arrived(here, gy_rsem.at[b, d])
-            share(here, gf_rsem.at[d])
-        for d in (1, 3, 2):
-            scale(b, from_y(d), c)
+            scaled[k] = times(gall.at[k])
+        if b == 0:
+            return
+        n = b - 1
+        both = lax.dot_general(
+            lhs[...].reshape(256, WIDTH), scaled[pl.ds(2 * n, 2)].reshape(256, WIDTH), nt,
+            preferred_element_type=F32,
+        ).astype(BF16)
+        for q in range(2):
+            tile = both[:128, LANES * q:LANES * (q + 1)].reshape(NZ, HALF, LANES)
+            out_s[0, :, :, pl.ds(column(2 * n + q), LANES)] = tile
+        lhs2[:, pl.ds(256 * n, 256)] = both[128:]
 
     def pass_roots(i, half):
         own = half.at[:, y, c]
@@ -244,6 +256,16 @@
             y_send(d, own, ry_rsem.at[i, d], 7)
         share(own, rf_rsem.at[i], 8)
 
+    for b in range(5):
+        for d in (1, 3, 2):
+            here = gall.at[batch(b), from_y(d), c]
+            arrived(here, gy_rsem.at[b, d])
+            share(here, gf_rsem.at[b])
+        if b:
+            whole(b - 1)
+    pass_roots(0, rh)
+    whole(4)
+
     def gathered(i, half):
         for d in (1, 3, 2):
             here = half.at[:, from_y(d), c]
@@ -251,40 +273,27 @@
             share(here, rf_rsem.at[i], 8)
         arrived(half.at[:, :, oc], rf_rsem.at[i])
 
-    pass_roots(0, rh)
-
-    for d in (0, 1, 3, 2):
-        arrived(gall.at[:, from_y(d), oc], gf_rsem.at[d])
-        for b in range(5):
-            scale(b, from_y(d), oc)
-    lhs[pl.ds(0, 128), :] = scaled[:, y, c].reshape(128, WIDTH)
-
     def o_sends(k):
         for d in ORDER[1:]:
             z_send(d, out_s.at[k], out_r[k].at[z, c], z_rsem.at[6 + k])
         out_r[k][z, c] = out_s[k, z]
 
-    nt = (((1,), (1,)), ((), ()))
-    for n in range(4):
-        g_rows = scaled[pl.ds(2 * n, 2)].reshape(256, WIDTH)
-        both = lax.dot_general(lhs[...], g_rows, nt, preferred_element_type=F32).astype(BF16)
-        out_s[0, :, :, pl.ds(256 * n, 256)] = both[:128].reshape(NZ, HALF, 256)
-        lhs2[:, pl.ds(256 * n, 256)] = both[128:]
     o_sends(0)
     for n in range(4):
         g_cols = scaled[:, :, :, :, pl.ds(256 * n, 256)].reshape(WIDTH, 256)
         both = jnp.dot(lhs2[...], g_cols, preferred_element_type=F32).astype(BF16)
         out_s[1, :, :, pl.ds(256 * n, 256)] = both.reshape(NZ, HALF, 256)
     o_sends(1)
-    gathered(0, rh)
-    unfold(rh, rfull)
     arrived(lmine.at[pl.ds(0, NZ - 1)], z_rsem.at[5])
-    left = lmine[...].reshape(128, WIDTH)
+    for k in range(NZ):
+        left[:, :, pl.ds(LANES * k, LANES)] = lmine[:, :, pl.ds(column(k), LANES)]
     for n in range(4):
         g_cols = scaled[:, :, :, :, pl.ds(256 * n, 256)].reshape(WIDTH, 256)
         app[:, pl.ds(256 * n, 256)] = jnp.dot(
-            left, g_cols, preferred_element_type=F32
+            left[...].reshape(128, WIDTH), g_cols, preferred_element_type=F32
         ).astype(BF16)
+    gathered(0, rh)
+    unfold(rh, rfull)
     for n in range(4):
         r_cols = rfull[:, :, :, :, pl.ds(256 * n, 256)].reshape(WIDTH, 256)
         upd = jnp.dot(app[...], r_cols, preferred_element_type=F32).astype(BF16)
@@ -341,6 +350,35 @@
     departed(norm_w, 4)
     departed(gall.at[pl.ds(0, 3)], 5)
     for copy in (done_left, done_right, done_upd):
+        copy.wait()
+
+
+def hand_over(*refs):
+    sems = refs[9]
+    pieces = [(i, n) for i in range(3) for n in range(2)]
+    halves = [refs[i].shape[0] // 2 for i in range(3)]
+
+    def part(i, n):
+        return pl.ds(n * halves[i], halves[i])
+
+    loads = [
+        pltpu.make_async_copy(
+            refs[i].at[part(i, n)], refs[6 + i].at[part(i, n)], sems.at[0, i, n]
+        )
+        for i, n in pieces
+    ]
+    stores = [
+        pltpu.make_async_copy(
+            refs[6 + i].at[part(i, n)], refs[3 + i].at[part(i, n)], sems.at[1, i, n]
+        )
+        for i, n in pieces
+    ]
+    for copy in loads:
+        copy.start()
+    for load, store in zip(loads, stores):
+        load.wait()
+        store.start()
+    for copy in stores:
         copy.wait()
 
 
@@ -371,8 +409,9 @@
             vmem((NZ, NY, 2, HALF, WEDGE * LANES), BF16),
             vmem((NZ, NY, 2, HALF, WIDTH), BF16),
             vmem((NZ, NY, 2, HALF, WIDTH), BF16),
-            vmem((256, WIDTH), BF16),
+            vmem((2 * NZ, HALF, WIDTH), BF16),
             vmem((128, WIDTH), BF16),
+            vmem((NZ, HALF, WIDTH), BF16),
             vmem((128, WIDTH), BF16),
             vmem((NY, 8, 128), F32),
             vmem((NX, 8, 128), F32),
@@ -390,7 +429,7 @@
             dma((9,)),
             dma((5, NY)),
             dma((1, NY)),
-            dma((NY,)),
+            dma((5,)),
             dma((1,)),
             dma((4,)),
             dma((3,)),
@@ -408,6 +447,23 @@
         left_roots.reshape(stat_shape),
         right_roots.reshape(stat_shape),
     )
+    new_left, new_right, updates = pl.pallas_call(
+        hand_over,
+        out_shape=[
+            jax.ShapeDtypeStruct(stat_shape, F32),
+            jax.ShapeDtypeStruct(stat_shape, F32),
+            jax.ShapeDtypeStruct((KF, 2, HALF, WIDTH), BF16),
+        ],
+        in_specs=[any_space] * 3,
+        out_specs=[any_space] * 3,
+        scratch_shapes=[
+            vmem(stat_shape, F32),
+            vmem(stat_shape, F32),
+            vmem((KF, 2, HALF, WIDTH), BF16),
+            dma((2, 3, 2)),
+        ],
+        compiler_params=pltpu.CompilerParams(vmem_limit_bytes=60 * 2**20),
+    )(new_left, new_right, updates)
     full = (1, 1, SLOTS, 2 * HALF, WIDTH)
     return (
         new_left.reshape(full),

time: 56.3 us -> 54.4 us (0.966)
  local copies, waits for them, and re-layouts: 4.28 us -> 0 us
  Pallas kernels: 50.8 us -> 53.2 us
    unnamed x7 -> x0, local copies, waits for them, and re-layouts: 4.28 us -> none
    pallas_call x0 -> x1, Pallas kernels: none -> 2.41 us  [on_device(): pl.pallas_call(hand_over, out_shape=[jax.ShapeDtypeStruct(stat_shape, F32...]
where the time goes in v4:
time: 54.4 us; the launch traced here: 53.8 us
  Pallas kernels  53.2 us (98%)
  between operations  0.64 us (1%)
    pallas_call x1, Pallas kernels, on_device(): pl.pallas_call(kernel, out_shape=[jax.ShapeDtypeStruct(stat_shape, F32),...  50.8 us
    pallas_call x1, Pallas kernels, on_device(): pl.pallas_call(hand_over, out_shape=[jax.ShapeDtypeStruct(stat_shape, F32...  2.41 us

profile of v4, /device:TPU:1, one launch (start us, length us, event | category | flops | bytes accessed | tf_op | source)
XLA Modules:
  0.0 53.8 jit_solution(14282100833497084055)
XLA Ops:
  0.6 50.8 %shard_map.85 = (f32[6,2,16,1024]{3,2,1,0:T(8,128)}, f32[6,2,16,1024]{3,2,1,0:T(8,128)}, bf16[8,2,16,1024]{3,2,1,0:T(8,128)(2,1)}) custom-call(s32[1,8]{1,0:T(1,128)} %owner_hbm.1, bf16[8,2,16,1024]{3,2,1,0:T(8,128)(2,1)} %bitcast.10, f32[6,2,16,1024]{3,2,1,0:T(8,128)} %bitcast.8, f32[6,2,16,1024]{3,2,1,0:T(8,128)} %bitcast.9, ...), custom_call_target="tpu_custom_call" | custom-call | tf_op jit(solution)/shard_map/pallas_call | solution.py:389
  51.4 2.4 %shard_map.86 = (f32[6,2,16,1024]{3,2,1,0:T(8,128)}, f32[6,2,16,1024]{3,2,1,0:T(8,128)}, bf16[8,2,16,1024]{3,2,1,0:T(8,128)(2,1)}) custom-call(f32[6,2,16,1024]{3,2,1,0:T(8,128)} %get-tuple-element.9.refs_0_, f32[6,2,16,1024]{3,2,1,0:T(8,128)} %get-tuple-element.10.refs_1_, bf16[8,2,16,1024]{3,2,1,0:T(8,128)(2,1)} %get-tuple-element.11.refs_2_), custom_call_target="tpu_custom_call" | custom-call | tf_op jit(solution)/shard_map/pallas_call | solution.py:450

commit v5 on v4

--- a/solution.py
+++ b/solution.py
@@ -21,6 +21,7 @@
 SLOTS = 6
 ORDER = (0, 1, 7, 2, 6, 3, 5, 4)
 BATCHES = ((0, 1), (1, 2), (3, 2), (5, 2), (7, 1))
+LEFT_RUNS = ((0, 1), (1, 1), (2, 1), (3, 1))
 BF16 = jnp.bfloat16
 F32 = jnp.float32
 
@@ -31,7 +32,7 @@
     owner_ref, own_g, got_g, part, lboth, rboth, lpart, rpart, lmine,
     gall, rh, scaled, rfull, lhs, lhs2, left, app,
     norm_y, norm_x, norm_c, norm_z, norm_w,
-    out_s, out_r0, out_r1, out_r2, lst, rst,
+    left_s, out_s, out_r0, out_r1, out_r2, lst, rst,
     loc_sem, c_rsem, z_rsem, gy_rsem, ry_rsem, gf_rsem, rf_rsem, n_rsem, o_rsem, fin_sem, s_sem,
 ):
     out_r = (out_r0, out_r1, out_r2)
@@ -245,9 +246,17 @@
             preferred_element_type=F32,
         ).astype(BF16)
         for q in range(2):
-            tile = both[:128, LANES * q:LANES * (q + 1)].reshape(NZ, HALF, LANES)
-            out_s[0, :, :, pl.ds(column(2 * n + q), LANES)] = tile
+            tile = both[:128, LANES * q:LANES * (q + 1)]
+            left_s[n, :, q] = tile.reshape(NZ, HALF, LANES)
         lhs2[:, pl.ds(256 * n, 256)] = both[128:]
+        for first, count in LEFT_RUNS:
+            if first + count == b:
+                runs = pl.ds(first, count)
+                for d in ORDER[1:]:
+                    remote(
+                        left_s.at[runs, lax.rem(z + d, NZ)], out_r0.at[runs, z, c],
+                        1, z_rsem.at[6], at_z(d),
+                    ).start()
 
     def pass_roots(i, half):
         own = half.at[:, y, c]
@@ -278,7 +287,7 @@
             z_send(d, out_s.at[k], out_r[k].at[z, c], z_rsem.at[6 + k])
         out_r[k][z, c] = out_s[k, z]
 
-    o_sends(0)
+    out_r0[:, z, c] = left_s[:, z]
     for n in range(4):
         g_cols = scaled[:, :, :, :, pl.ds(256 * n, 256)].reshape(WIDTH, 256)
         both = jnp.dot(lhs2[...], g_cols, preferred_element_type=F32).astype(BF16)
@@ -312,6 +321,18 @@
 
     mix = (1.0 - STAT_DECAY) / WIDTH
 
+    def finish_left():
+        arrived(out_r0.at[:, pl.ds(0, NZ - 1), c], z_rsem.at[6])
+        here = out_r0.at[:, :, c]
+        remote(here, here, 5, o_rsem.at[0], at_c(1)).start()
+        arrived(out_r0.at[:, :, oc], o_rsem.at[0])
+
+    def left_gram(s, block):
+        far = lax.rem(places[s] + NZ - block, NZ)
+        pair = jnp.where(far > 4, NZ - far, jnp.maximum(far - 1, 0))
+        second = jnp.where((far > 0) & (far < 5), 1, 0)
+        return out_r0[pair, places[s], :, second]
+
     def finish(k):
         arrived(out_r[k].at[pl.ds(0, NZ - 1), c], z_rsem.at[6 + k])
         here = out_r[k].at[:, c]
@@ -320,7 +341,10 @@
 
     def stats(k, buf, out_ref):
         for s in range(SLOTS):
-            gram = out_r[k][places[s]].astype(F32)
+            if k == 0:
+                gram = jnp.concatenate([left_gram(s, b) for b in range(NZ)], axis=-1).astype(F32)
+            else:
+                gram = out_r[k][places[s]].astype(F32)
             new = STAT_DECAY * buf[s] + mix * gram
             buf[s] = jnp.where(taken[s] > 0, new, buf[s])
         copy = pltpu.make_async_copy(buf, out_ref, fin_sem.at[k])
@@ -328,7 +352,7 @@
         return copy
 
     local[4].wait()
-    finish(0)
+    finish_left()
     done_left = stats(0, lst, nleft_ref)
     local[5].wait()
     finish(1)
@@ -418,8 +442,9 @@
             vmem((2, 8, 128), F32),
             vmem((NZ, 8, 128), F32),
             vmem((14, 8, 128), F32),
+            vmem((4, NZ, 2, HALF, LANES), BF16),
             vmem((3, NZ, HALF, WIDTH), BF16),
-            vmem((KF, 2, HALF, WIDTH), BF16),
+            vmem((4, KF, 2, 2, HALF, LANES), BF16),
             vmem((KF, 2, HALF, WIDTH), BF16),
             vmem((KF, 2, HALF, WIDTH), BF16),
             vmem(stat_shape, F32),

time: 54.4 us -> 53.1 us (0.976)
  Pallas kernels: 53.2 us -> 52.3 us
    pallas_call x1, Pallas kernels: 50.8 us -> 49.9 us  [on_device(): pl.pallas_call(kernel, out_shape=[jax.ShapeDtypeStruct(stat_shape, F32),...]
where the time goes in v5:
time: 53.1 us; the launch traced here: 53 us
  Pallas kernels  52.3 us (98%)
  between operations  0.64 us (1%)
    pallas_call x1, Pallas kernels, on_device(): pl.pallas_call(kernel, out_shape=[jax.ShapeDtypeStruct(stat_shape, F32),...  49.9 us
    pallas_call x1, Pallas kernels, on_device(): pl.pallas_call(hand_over, out_shape=[jax.ShapeDtypeStruct(stat_shape, F32...  2.41 us

profile of v5, /device:TPU:1, one launch (start us, length us, event | category | flops | bytes accessed | tf_op | source)
XLA Modules:
  0.0 53.0 jit_solution(14363141122587213007)
XLA Ops:
  0.6 49.9 %shard_map.85 = (f32[6,2,16,1024]{3,2,1,0:T(8,128)}, f32[6,2,16,1024]{3,2,1,0:T(8,128)}, bf16[8,2,16,1024]{3,2,1,0:T(8,128)(2,1)}) custom-call(s32[1,8]{1,0:T(1,128)} %owner_hbm.1, bf16[8,2,16,1024]{3,2,1,0:T(8,128)(2,1)} %bitcast.10, f32[6,2,16,1024]{3,2,1,0:T(8,128)} %bitcast.8, f32[6,2,16,1024]{3,2,1,0:T(8,128)} %bitcast.9, ...), custom_call_target="tpu_custom_call" | custom-call | tf_op jit(solution)/shard_map/pallas_call | solution.py:413
  50.6 2.4 %shard_map.86 = (f32[6,2,16,1024]{3,2,1,0:T(8,128)}, f32[6,2,16,1024]{3,2,1,0:T(8,128)}, bf16[8,2,16,1024]{3,2,1,0:T(8,128)(2,1)}) custom-call(f32[6,2,16,1024]{3,2,1,0:T(8,128)} %get-tuple-element.9.refs_0_, f32[6,2,16,1024]{3,2,1,0:T(8,128)} %get-tuple-element.10.refs_1_, bf16[8,2,16,1024]{3,2,1,0:T(8,128)(2,1)} %get-tuple-element.11.refs_2_), custom_call_target="tpu_custom_call" | custom-call | tf_op jit(solution)/shard_map/pallas_call | solution.py:475

commit v6 on v5

--- a/solution.py
+++ b/solution.py
@@ -307,7 +307,14 @@
         r_cols = rfull[:, :, :, :, pl.ds(256 * n, 256)].reshape(WIDTH, 256)
         upd = jnp.dot(app[...], r_cols, preferred_element_type=F32).astype(BF16)
         out_s[2, :, :, pl.ds(256 * n, 256)] = upd.reshape(NZ, HALF, 256)
-    o_sends(2)
+        if n % 2:
+            run = pl.ds(256 * (n - 1), 512)
+            for d in ORDER[1:]:
+                remote(
+                    out_s.at[2, lax.rem(z + d, NZ), :, run], out_r2.at[z, c, :, run],
+                    1, z_rsem.at[8], at_z(d),
+                ).start()
+    out_r2[z, c] = out_s[2, z]
 
     places, taken = [], []
     for s in range(SLOTS):

time: 53.1 us -> 53.6 us (level)
  no operation moved by 1% of the time
where the time goes in v6:
time: 53.6 us; the launch traced here: 53.4 us
  Pallas kernels  52.8 us (99%)
  between operations  0.64 us (1%)
    pallas_call x1, Pallas kernels, on_device(): pl.pallas_call(kernel, out_shape=[jax.ShapeDtypeStruct(stat_shape, F32),...  50.4 us
    pallas_call x1, Pallas kernels, on_device(): pl.pallas_call(hand_over, out_shape=[jax.ShapeDtypeStruct(stat_shape, F32...  2.41 us

profile of v6, /device:TPU:1, one launch (start us, length us, event | category | flops | bytes accessed | tf_op | source)
XLA Modules:
  0.0 53.4 jit_solution(837488068916054257)
XLA Ops:
  0.6 50.4 %shard_map.85 = (f32[6,2,16,1024]{3,2,1,0:T(8,128)}, f32[6,2,16,1024]{3,2,1,0:T(8,128)}, bf16[8,2,16,1024]{3,2,1,0:T(8,128)(2,1)}) custom-call(s32[1,8]{1,0:T(1,128)} %owner_hbm.1, bf16[8,2,16,1024]{3,2,1,0:T(8,128)(2,1)} %bitcast.10, f32[6,2,16,1024]{3,2,1,0:T(8,128)} %bitcast.8, f32[6,2,16,1024]{3,2,1,0:T(8,128)} %bitcast.9, ...), custom_call_target="tpu_custom_call" | custom-call | tf_op jit(solution)/shard_map/pallas_call | solution.py:420
  51.0 2.4 %shard_map.86 = (f32[6,2,16,1024]{3,2,1,0:T(8,128)}, f32[6,2,16,1024]{3,2,1,0:T(8,128)}, bf16[8,2,16,1024]{3,2,1,0:T(8,128)(2,1)}) custom-call(f32[6,2,16,1024]{3,2,1,0:T(8,128)} %get-tuple-element.9.refs_0_, f32[6,2,16,1024]{3,2,1,0:T(8,128)} %get-tuple-element.10.refs_1_, bf16[8,2,16,1024]{3,2,1,0:T(8,128)(2,1)} %get-tuple-element.11.refs_2_), custom_call_target="tpu_custom_call" | custom-call | tf_op jit(solution)/shard_map/pallas_call | solution.py:482
